TPU v7x, 32 devices: a whole 2x2x4 slice. The times are simulated.
32 devices in a mesh: dp: 2 (over x), context: 4 (over y, core), expert: 4 (over z).
Axes of the slice: x: 2, y: 2, z: 4, core: 2. Of those that a mesh axis runs over, the one named last changes fastest.
Arguments:
- prompt_in: bfloat16 [8, 1024, 768], P(('dp', 'expert'), 'context'), may hold values from -6 to 6
- cont_in: bfloat16 [8, 2, 512, 768], P(('dp', 'expert'), None, 'context'), may hold values from -6 to 6
- prompt_route: int32 [8, 1024, 2], P(('dp', 'expert'), 'context'), may hold values from 0 to 3, all different within a row
- cont_route: int32 [8, 2, 512, 2], P(('dp', 'expert'), None, 'context'), may hold values from 0 to 3, all different within a row
- order: int32 [8, 4, 512], P(('dp', 'expert'), 'context'), may hold values from 0 to 511, each once within a row
- buckets: int32 [1536], replicated, may hold values from 0 to 31
- attn_gain: float32 [768], replicated, may hold values from 0.1 to 1.9
- w_query: bfloat16 [768, 768], replicated, may hold values from -0.21875 to 0.21875
- w_key: bfloat16 [768, 768], replicated, may hold values from -0.21875 to 0.21875
- w_value: bfloat16 [768, 768], replicated, may hold values from -0.21875 to 0.21875
- w_attn_out: bfloat16 [768, 768], replicated, may hold values from -0.625 to 0.625
- rel_bias: float32 [32, 12], replicated, may hold values from -4 to 4
- ffn_gain: float32 [768], replicated, may hold values from 0.1 to 1.9
- router: bfloat16 [768, 4], replicated, may hold values from -0.109375 to 0.109375
- w_in: bfloat16 [4, 768, 3072], P('expert'), may hold values from -0.21875 to 0.21875
- w_out: bfloat16 [4, 3072, 768], P('expert'), may hold values from -0.21875 to 0.21875
- prompt_cot: bfloat16 [8, 1024, 768], P(('dp', 'expert'), 'context'), may hold values from -6 to 6
- cont_cot: bfloat16 [8, 2, 512, 768], P(('dp', 'expert'), None, 'context'), may hold values from -6 to 6
Outputs:
- prompt_out: bfloat16 [8, 1024, 768], P(('dp', 'expert'), 'context')
- cont_out: bfloat16 [8, 2, 512, 768], P(('dp', 'expert'), None, 'context')
- prompt_dx: float32 [8, 1024, 768], P(('dp', 'expert'), 'context')
- cont_dx: float32 [8, 2, 512, 768], P(('dp', 'expert'), None, 'context')
- g_attn_gain: float32 [768], replicated
- g_w_query: float32 [768, 768], replicated
- g_w_key: float32 [768, 768], replicated
- g_w_value: float32 [768, 768], replicated
- g_w_attn_out: float32 [768, 768], replicated
- g_rel_bias: float32 [32, 12], replicated
- g_ffn_gain: float32 [768], replicated
- g_router: float32 [768, 4], replicated
- g_w_in: float32 [4, 768, 3072], P('expert', ('dp', 'context'))
- g_w_out: float32 [4, 3072, 768], P('expert', ('dp', 'context'))
Inputs may be any that keep to these rules, and one draw needn't show every extreme that they name: `prompt_route`: each token's 2 experts differ. `cont_route`: each token's 2 experts differ. `order`: each block's row lists each of its 512 tokens once.
All inputs are finite; a program needn't handle non-finite values.
Results may differ from a plain program's by a relative error of at most 0.015.
Values may be sent and summed in bfloat16 or wider, within the bound.
A program may use at most 384 MiB of HBM per device.

v0:
```python
import jax
import jax.numpy as jnp
from jax import lax
from jax.sharding import PartitionSpec as P

HD = 64
NB = 32


EPSILON = 1e-06
PRECISE = lax.Precision.HIGHEST
MASKED = -1e30


def rms_scale(values, gain):
    return values * lax.rsqrt(jnp.mean(values * values, axis=-1, keepdims=True) + EPSILON) * gain


def gelu_tanh(values):
    return jax.nn.gelu(values, approximate=True)


def slot_plan(route, ranking, experts, capacity):
    rows_count = route.shape[0]
    top_k = route.shape[1]
    ranked = route[ranking]
    flat_route = ranked.T.reshape(-1)
    hot_rows = (flat_route[:, None] == jnp.arange(experts, dtype=jnp.int32)[None, :]).astype(
        jnp.int32
    )
    position = jnp.sum((jnp.cumsum(hot_rows, axis=0) - hot_rows) * hot_rows, axis=1)
    slot_index = jnp.where(
        position < capacity, flat_route * capacity + position, experts * capacity
    )
    pick_index = jnp.arange(top_k * rows_count, dtype=jnp.int32) // rows_count
    anchor = jnp.tile(ranking, top_k) * top_k + pick_index
    destination = (
        jnp.zeros((rows_count * top_k,), jnp.int32)
        .at[anchor]
        .set(slot_index)
        .reshape(rows_count, top_k)
    )
    source = (
        jnp.full((experts * capacity + 1,), rows_count * top_k, jnp.int32)
        .at[slot_index]
        .set(anchor)[: experts * capacity]
    )
    return (destination, source)


def token_meta(device, local, prompt_rows, cont_rows, prompt_len):
    in_prompt = local < prompt_rows
    after = jnp.maximum(local - prompt_rows, 0)
    sequence = jnp.where(in_prompt, -1, after // cont_rows)
    position = jnp.where(
        in_prompt, device * prompt_rows + local, prompt_len + device * cont_rows + after % cont_rows
    )
    return (position, sequence)


def split_pairs(matrix, pair_width):
    return matrix.reshape(matrix.shape[0], -1, pair_width).transpose(1, 0, 2)


def join_pairs(stacked):
    return stacked.transpose(1, 0, 2).reshape(stacked.shape[1], -1)


def two_heads(matrix):
    return matrix.reshape(matrix.shape[0], 2, -1)


def toeplitz_tile(vector, rows, cols):
    heads = vector.shape[0]
    width = rows + cols
    extended = jnp.concatenate([vector[:, ::-1], jnp.zeros((heads, 1), vector.dtype)], axis=1)
    rotated = jnp.concatenate([extended[:, rows - 1 :], extended[:, : rows - 1]], axis=1)
    flat = jnp.tile(rotated, (1, rows))[:, : rows * (width - 1)]
    return flat.reshape(heads, rows, width - 1)[:, :, :cols]


def diagonal_sums(tile, rows, cols):
    heads = tile.shape[0]
    width = rows + cols
    padded = jnp.concatenate([tile, jnp.zeros((heads, rows, width - 1 - cols), tile.dtype)], axis=2)
    flat = padded.reshape(heads, rows * (width - 1))
    flat = jnp.concatenate([flat, jnp.zeros((heads, rows), tile.dtype)], axis=1)
    rotated = jnp.sum(flat.reshape(heads, rows, width), axis=1)
    cut = width - (rows - 1)
    extended = jnp.concatenate([rotated[:, cut:], rotated[:, :cut]], axis=1)
    return extended[:, : width - 1][:, ::-1]


def build_bias(table_ext, query_groups, key_groups, query_total, key_total, span):
    heads = table_ext.shape[0]
    result = jnp.zeros((heads, query_total, key_total), jnp.float32)
    for q_start, q_len, q_offsets in query_groups:
        for k_start, k_len, k_offsets in key_groups:
            begin = q_start - k_start - (k_len - 1) + span
            vector = lax.dynamic_slice_in_dim(table_ext, begin, q_len + k_len - 1, 1)
            tile = toeplitz_tile(vector, q_len, k_len)
            for q_off in q_offsets:
                for k_off in k_offsets:
                    result = result.at[:, q_off : q_off + q_len, k_off : k_off + k_len].set(tile)
    return result


def distance_grad(grad_scores, query_groups, key_groups, span):
    heads = grad_scores.shape[0]
    grad_full = grad_scores.astype(jnp.float32)
    total = jnp.zeros((heads, 2 * span), jnp.float32)
    for q_start, q_len, q_offsets in query_groups:
        for k_start, k_len, k_offsets in key_groups:
            tile = jnp.zeros((heads, q_len, k_len), jnp.float32)
            for q_off in q_offsets:
                for k_off in k_offsets:
                    tile = tile + grad_full[:, q_off : q_off + q_len, k_off : k_off + k_len]
            sums = diagonal_sums(tile, q_len, k_len)
            begin = q_start - k_start - (k_len - 1) + span
            current = lax.dynamic_slice_in_dim(total, begin, q_len + k_len - 1, 1)
            total = lax.dynamic_update_slice_in_dim(total, current + sums, begin, 1)
    return total


def pair_scores(query_pair, key_pair, bias_block, allowed, score_scale):
    raw = (
        jnp.einsum(
            "qhd,khd->hqk",
            two_heads(query_pair),
            two_heads(key_pair),
            preferred_element_type=jnp.float32,
        )
        * score_scale
    )
    return jnp.where(allowed[None], raw + bias_block, MASKED)


def pair_backward(
    query_pair,
    key_pair,
    value_pair,
    grad_pair,
    lse_pair,
    bias_block,
    allowed,
    delta_pair,
    score_scale,
):
    scores = pair_scores(query_pair, key_pair, bias_block, allowed, score_scale)
    probability = jnp.exp(scores - lse_pair[:, :, None])
    grad_probs = jnp.einsum(
        "qhd,khd->hqk",
        two_heads(grad_pair),
        two_heads(value_pair),
        preferred_element_type=jnp.float32,
    )
    delta_pair = jnp.sum(probability * grad_probs, axis=-1)
    grad_scores = (probability * (grad_probs - delta_pair[:, :, None])).astype(jnp.bfloat16)
    return (probability, grad_scores, delta_pair)


def body(
    prompt_in,
    cont_in,
    prompt_route,
    cont_route,
    order,
    buckets,
    attn_gain,
    w_query,
    w_key,
    w_value,
    w_attn_out,
    rel_bias,
    ffn_gain,
    router,
    w_in,
    w_out,
    prompt_cot,
    cont_cot,
):
    prompt_rows = prompt_in.shape[1]
    cont_count = cont_in.shape[1]
    cont_rows = cont_in.shape[2]
    model_width = prompt_in.shape[2]
    spread = lax.axis_size("context")
    tokens = prompt_rows + cont_count * cont_rows
    prompt_len = prompt_rows * spread
    span = prompt_len + cont_rows * spread
    pair_width = 2 * HD
    score_scale = HD ** (-0.5)
    head_count = rel_bias.shape[1]

    def local_rows(prompt_part, cont_part):
        return jnp.concatenate(
            [prompt_part.reshape(prompt_rows, -1), cont_part.reshape(cont_count * cont_rows, -1)],
            axis=0,
        )

    hidden = local_rows(prompt_in, cont_in).astype(jnp.float32)
    routes = local_rows(prompt_route, cont_route)
    upstream = local_rows(prompt_cot, cont_cot).astype(jnp.float32)
    ranking = order.reshape(tokens)
    device = lax.axis_index("context")
    local_index = jnp.arange(tokens, dtype=jnp.int32)
    here_pos, here_seq = token_meta(device, local_index, prompt_rows, cont_rows, prompt_len)
    every_index = jnp.arange(spread * tokens, dtype=jnp.int32)
    every_pos, every_seq = token_meta(
        every_index // tokens, every_index % tokens, prompt_rows, cont_rows, prompt_len
    )
    allowed = ((every_seq[None, :] < 0) | (every_seq[None, :] == here_seq[:, None])) & (
        every_pos[None, :] <= here_pos[:, None]
    )
    cont_offsets = [prompt_rows + j * cont_rows for j in range(cont_count)]
    here_groups = [
        (device * prompt_rows, prompt_rows, [0]),
        (prompt_len + device * cont_rows, cont_rows, cont_offsets),
    ]
    every_groups = []
    for other in range(spread):
        every_groups.append((other * prompt_rows, prompt_rows, [other * tokens]))
        every_groups.append(
            (prompt_len + other * cont_rows, cont_rows, [other * tokens + c for c in cont_offsets])
        )
    bucket_hot = (buckets[:, None] == jnp.arange(NB, dtype=jnp.int32)[None, :]).astype(jnp.float32)
    table = jnp.dot(bucket_hot, rel_bias, precision=PRECISE).T
    table_ext = jnp.concatenate([jnp.zeros((head_count, span), jnp.float32), table], axis=1)
    bias_here = build_bias(table_ext, here_groups, every_groups, tokens, spread * tokens, span)
    bias_here = bias_here.reshape(head_count // 2, 2, tokens, spread * tokens)
    normed = rms_scale(hidden, attn_gain).astype(jnp.bfloat16)
    queries = jnp.dot(normed, w_query, preferred_element_type=jnp.float32).astype(jnp.bfloat16)
    key_rows = jnp.dot(normed, w_key, preferred_element_type=jnp.float32).astype(jnp.bfloat16)
    value_rows = jnp.dot(normed, w_value, preferred_element_type=jnp.float32).astype(jnp.bfloat16)
    keys_all, values_all = (
        lax.all_gather(key_rows, "context", axis=0, tiled=True),
        lax.all_gather(value_rows, "context", axis=0, tiled=True),
    )
    query_pairs = split_pairs(queries, pair_width)
    key_pairs = split_pairs(keys_all, pair_width)
    value_pairs = split_pairs(values_all, pair_width)

    def forward_pair(pair_items):
        query_pair, key_pair, value_pair, bias_block = pair_items
        scores = pair_scores(query_pair, key_pair, bias_block, allowed, score_scale)
        largest = jnp.max(scores, axis=-1, keepdims=True)
        powered = jnp.exp(scores - largest)
        totals = jnp.sum(powered, axis=-1, keepdims=True)
        probability = (powered / totals).astype(jnp.bfloat16)
        attended = jnp.einsum(
            "hqk,khd->qhd", probability, two_heads(value_pair), preferred_element_type=jnp.float32
        )
        return (attended.reshape(attended.shape[0], -1), (largest + jnp.log(totals))[..., 0])

    attended_pairs, log_totals = lax.map(
        forward_pair, (query_pairs, key_pairs, value_pairs, bias_here)
    )
    attended = join_pairs(attended_pairs).astype(jnp.bfloat16)
    middle = hidden + jnp.dot(attended, w_attn_out, preferred_element_type=jnp.float32)
    second = rms_scale(middle, ffn_gain).astype(jnp.bfloat16)
    second_full = second.astype(jnp.float32)
    local_experts = w_in.shape[0]
    expert_devices = lax.axis_size("expert")
    experts = local_experts * expert_devices
    top_k = routes.shape[1]
    capacity = 9 * tokens * top_k // (8 * experts)
    router_full = router.astype(jnp.float32)
    logits = jnp.dot(second_full, router_full, precision=PRECISE)
    route_hot = (routes[:, :, None] == jnp.arange(experts, dtype=jnp.int32)[None, None, :]).astype(
        jnp.float32
    )
    chosen = jnp.einsum("tke,te->tk", route_hot, logits, precision=PRECISE)
    gates = jax.nn.softmax(chosen, axis=-1)
    destination, source = slot_plan(routes, ranking, experts, capacity)
    padded = jnp.concatenate([second, jnp.zeros((1, model_width), jnp.bfloat16)], axis=0)
    outgoing = padded[source // top_k].reshape(
        expert_devices, local_experts * capacity, model_width
    )
    arrived = lax.all_to_all(outgoing, "expert", split_axis=0, concat_axis=0, tiled=True).reshape(
        expert_devices, local_experts, capacity, model_width
    )
    before = jnp.einsum("secd,edf->secf", arrived, w_in, preferred_element_type=jnp.float32)
    activated = gelu_tanh(before).astype(jnp.bfloat16)
    produced = jnp.einsum(
        "secf,efd->secd", activated, w_out, preferred_element_type=jnp.float32
    ).astype(jnp.bfloat16)
    returned = lax.all_to_all(
        produced.reshape(expert_devices, local_experts * capacity, model_width),
        "expert",
        split_axis=0,
        concat_axis=0,
        tiled=True,
    )
    returned = jnp.concatenate(
        [
            returned.reshape(experts * capacity, model_width),
            jnp.zeros((1, model_width), jnp.bfloat16),
        ],
        axis=0,
    )
    picked = returned[destination].astype(jnp.float32)
    final = middle + jnp.sum(gates[:, :, None] * picked, axis=1)
    grad_gates = jnp.sum(upstream[:, None, :] * picked, axis=2)
    grad_slots = (gates[:, :, None] * upstream[:, None, :]).reshape(tokens * top_k, model_width)
    grad_slots = jnp.concatenate([grad_slots, jnp.zeros((1, model_width), jnp.float32)], axis=0)
    grad_produced = (
        grad_slots[source]
        .astype(jnp.bfloat16)
        .reshape(expert_devices, local_experts * capacity, model_width)
    )
    grad_arrived = lax.all_to_all(
        grad_produced, "expert", split_axis=0, concat_axis=0, tiled=True
    ).reshape(expert_devices, local_experts, capacity, model_width)
    grad_activated = jnp.einsum(
        "secd,efd->secf", grad_arrived, w_out, preferred_element_type=jnp.float32
    )
    outer_grad = jnp.einsum(
        "secf,secd->efd", activated, grad_arrived, preferred_element_type=jnp.float32
    )
    unused, gelu_pull = jax.vjp(gelu_tanh, before)
    grad_before = gelu_pull(grad_activated)[0].astype(jnp.bfloat16)
    inner_grad = jnp.einsum(
        "secd,secf->edf", arrived, grad_before, preferred_element_type=jnp.float32
    )
    grad_sent = jnp.einsum(
        "secf,edf->secd", grad_before, w_in, preferred_element_type=jnp.float32
    ).astype(jnp.bfloat16)
    grad_back = lax.all_to_all(
        grad_sent.reshape(expert_devices, local_experts * capacity, model_width),
        "expert",
        split_axis=0,
        concat_axis=0,
        tiled=True,
    )
    grad_back = jnp.concatenate(
        [
            grad_back.reshape(experts * capacity, model_width),
            jnp.zeros((1, model_width), jnp.bfloat16),
        ],
        axis=0,
    )
    grad_second = jnp.sum(grad_back[destination].astype(jnp.float32), axis=1)
    grad_chosen = gates * (grad_gates - jnp.sum(gates * grad_gates, axis=1, keepdims=True))
    grad_logits = jnp.einsum("tke,tk->te", route_hot, grad_chosen, precision=PRECISE)
    grad_second = grad_second + jnp.dot(grad_logits, router_full.T, precision=PRECISE)
    router_grad = jnp.dot(second_full.T, grad_logits, precision=PRECISE)
    unused, second_pull = jax.vjp(rms_scale, middle, ffn_gain)
    grad_middle, ffn_gain_grad = second_pull(grad_second)
    grad_middle = grad_middle + upstream
    grad_branch = grad_middle.astype(jnp.bfloat16)
    attn_out_grad = jnp.dot(attended.T, grad_branch, preferred_element_type=jnp.float32)
    grad_attended = jnp.dot(grad_branch, w_attn_out.T, preferred_element_type=jnp.float32).astype(
        jnp.bfloat16
    )
    grad_pairs = split_pairs(grad_attended, pair_width)

    def backward_pair(pair_items):
        query_pair, key_pair, value_pair, grad_pair, lse_pair, bias_block = pair_items
        probability, grad_scores, delta_pair = pair_backward(
            query_pair,
            key_pair,
            value_pair,
            grad_pair,
            lse_pair,
            bias_block,
            allowed,
            None,
            score_scale,
        )
        grad_query = (
            jnp.einsum(
                "hqk,khd->qhd", grad_scores, two_heads(key_pair), preferred_element_type=jnp.float32
            )
            * score_scale
        )
        grad_key = (
            jnp.einsum(
                "hqk,qhd->khd",
                grad_scores,
                two_heads(query_pair),
                preferred_element_type=jnp.float32,
            )
            * score_scale
        )
        grad_value = jnp.einsum(
            "hqk,qhd->khd",
            probability.astype(jnp.bfloat16),
            two_heads(grad_pair),
            preferred_element_type=jnp.float32,
        )
        return (
            grad_query.reshape(grad_query.shape[0], -1),
            grad_key.reshape(grad_key.shape[0], -1),
            grad_value.reshape(grad_value.shape[0], -1),
            distance_grad(grad_scores, here_groups, every_groups, span),
        )

    grad_query_pairs, grad_key_pairs, grad_value_pairs, distance_sums = lax.map(
        backward_pair, (query_pairs, key_pairs, value_pairs, grad_pairs, log_totals, bias_here)
    )
    grad_key_rows, grad_value_rows = (
        lax.psum_scatter(
            join_pairs(grad_key_pairs).astype(jnp.bfloat16),
            "context",
            scatter_dimension=0,
            tiled=True,
        ).astype(jnp.float32),
        lax.psum_scatter(
            join_pairs(grad_value_pairs).astype(jnp.bfloat16),
            "context",
            scatter_dimension=0,
            tiled=True,
        ).astype(jnp.float32),
    )
    grad_queries = join_pairs(grad_query_pairs).astype(jnp.bfloat16)
    grad_keys = grad_key_rows.astype(jnp.bfloat16)
    grad_values = grad_value_rows.astype(jnp.bfloat16)
    query_grad = jnp.dot(normed.T, grad_queries, preferred_element_type=jnp.float32)
    key_grad = jnp.dot(normed.T, grad_keys, preferred_element_type=jnp.float32)
    value_grad = jnp.dot(normed.T, grad_values, preferred_element_type=jnp.float32)
    grad_normed = jnp.dot(grad_queries, w_query.T, preferred_element_type=jnp.float32)
    grad_normed = grad_normed + jnp.dot(grad_keys, w_key.T, preferred_element_type=jnp.float32)
    grad_normed = grad_normed + jnp.dot(grad_values, w_value.T, preferred_element_type=jnp.float32)
    unused, first_pull = jax.vjp(rms_scale, hidden, attn_gain)
    grad_hidden, attn_gain_grad = first_pull(grad_normed)
    grad_hidden = grad_hidden + grad_middle
    distance_all = distance_sums.reshape(head_count, 2 * span)[:, span:]
    bias_grad = jnp.dot(distance_all, bucket_hot, precision=PRECISE).T
    summed = lax.psum(
        (
            attn_gain_grad,
            query_grad,
            key_grad,
            value_grad,
            attn_out_grad,
            bias_grad,
            ffn_gain_grad,
            router_grad,
        ),
        ("dp", "context", "expert"),
    )
    inner_sum, outer_sum = (
        lax.psum_scatter(
            inner_grad.astype(jnp.bfloat16), ("dp", "context"), scatter_dimension=1, tiled=True
        ).astype(jnp.float32),
        lax.psum_scatter(
            outer_grad.astype(jnp.bfloat16), ("dp", "context"), scatter_dimension=1, tiled=True
        ).astype(jnp.float32),
    )
    prompt_out = final[:prompt_rows].reshape(1, prompt_rows, model_width).astype(jnp.bfloat16)
    cont_out = (
        final[prompt_rows:].reshape(1, cont_count, cont_rows, model_width).astype(jnp.bfloat16)
    )
    prompt_dx = grad_hidden[:prompt_rows].reshape(1, prompt_rows, model_width)
    cont_dx = grad_hidden[prompt_rows:].reshape(1, cont_count, cont_rows, model_width)
    return (
        prompt_out,
        cont_out,
        prompt_dx,
        cont_dx,
        summed[0],
        summed[1],
        summed[2],
        summed[3],
        summed[4],
        summed[5],
        summed[6],
        summed[7],
        inner_sum,
        outer_sum,
    )


def solution(mesh):
    return jax.shard_map(
        body,
        mesh=mesh,
        in_specs=(
            P(("dp", "expert"), "context", None),
            P(("dp", "expert"), None, "context", None),
            P(("dp", "expert"), "context", None),
            P(("dp", "expert"), None, "context", None),
            P(("dp", "expert"), "context", None),
            P(),
            P(),
            P(),
            P(),
            P(),
            P(),
            P(),
            P(),
            P(),
            P("expert", None, None),
            P("expert", None, None),
            P(("dp", "expert"), "context", None),
            P(("dp", "expert"), None, "context", None),
        ),
        out_specs=(
            P(("dp", "expert"), "context", None),
            P(("dp", "expert"), None, "context", None),
            P(("dp", "expert"), "context", None),
            P(("dp", "expert"), None, "context", None),
            P(),
            P(),
            P(),
            P(),
            P(),
            P(),
            P(),
            P(),
            P("expert", ("dp", "context"), None),
            P("expert", ("dp", "context"), None),
        ),
        check_vma=False,
    )
```

profile of v0, /device:TPU:0, one launch (start us, length us, event | category | flops | bytes accessed | tf_op | source)
XLA Modules:
  0.0 1997.0 jit_solution(2267163000880719779)
XLA Ops:
  53.2 9.6 reshape.2122
  65.1 16.5 scatter.134
  85.5 17.0 scatter.135
  107.3 17.0 scatter.136
  135.5 9.5 reshape.2128
  155.4 31.9 %scatter.139 = f32[12,512,2048]{2,1,0:T(8,128)} dynamic-update-slice(f32[12,512,2048]{2,1,0:T(8,128)} %scatter.136, f32[12,256,256]{2,1,0:T(8,128)} %slice_select_fusion.2, s32[]{:T(128)} %constant.1445.clone.1, s32[]{:T(128)} %bitcast.13, s32[]{:T(128)} %bitcast.14) | dynamic-update-slice | bytes 6291460 | tf_op jit(solution)/shard_map/scatter | solution.py:104
  208.7 17.0 scatter.140
  230.3 16.7 scatter.141
  258.4 9.4 reshape.2136
  275.8 31.7 %scatter.144 = f32[12,512,2048]{2,1,0:T(8,128)} dynamic-update-slice(f32[12,512,2048]{2,1,0:T(8,128)} %scatter.141, f32[12,256,256]{2,1,0:T(8,128)} %slice_select_fusion.1, s32[]{:T(128)} %constant.1445.clone.1, s32[]{:T(128)} %bitcast.19, s32[]{:T(128)} %bitcast.20) | dynamic-update-slice | bytes 6291460 | tf_op jit(solution)/shard_map/scatter | solution.py:104
  328.9 17.0 scatter.145
  350.6 16.8 scatter.146
  378.6 9.3 reshape.2144
  395.6 31.8 %scatter.149 = f32[12,512,2048]{2,1,0:T(8,128)} dynamic-update-slice(f32[12,512,2048]{2,1,0:T(8,128)} %scatter.146, f32[12,256,256]{2,1,0:T(8,128)} %slice_select_fusion, s32[]{:T(128)} %constant.1445.clone.1, s32[]{:T(128)} %bitcast.25, s32[]{:T(128)} %bitcast.26) | dynamic-update-slice | bytes 6291460 | tf_op jit(solution)/shard_map/scatter | solution.py:104
  448.9 16.9 scatter.150
  470.1 15.8 scatter.151
  609.6 74.0 %while.69 = (s32[]{:T(128)}, bf16[6,512,128]{1,2,0:T(8,128)(2,1)S(1)}, f32[6,2,512]{2,1,0:T(2,128)}, bf16[6,2048,128]{1,2,0:T(8,128)(2,1)}, bf16[6,512,128]{1,2,...) while((s32[]{:T(128)}, ...), condition=%wide.region_15.16_spmd.clone, body=%wide.region_12.15_spmd.clone.sunk | while | flops 559938560 | bytes 39639692 | solution.py:254
  719.8 20.4 %all-to-all-done = bf16[4,288,768]{2,1,0:T(8,128)(2,1)} async-done(((bf16[4,288,768]{2,1,0:T(8,128)(2,1)}), bf16[4,288,768]{2,1,0:T(8,128)(2,1)}, u32[]{:S(2)}, u32[]{:S(2)}) %all-to-all-start) | async-done | bytes 1769504 | tf_op jit(solution)/shard_map/all_to_all | solution.py:278
  757.0 11.6 fusion.70
  768.7 15.8 all-to-all-done.2
  789.7 17.1 fusion.35
  809.7 9.2 fusion.75
  818.9 11.4 all-to-all-done.1
  855.0 9.4 multiply_reduce_fusion.1
  903.1 684.0 %while.70 = (s32[]{:T(128)}, bf16[6,512,128]{1,2,0:T(8,128)(2,1)}, bf16[6,2048,128]{1,2,0:T(8,128)(2,1)}, bf16[6,2048,128]{1,2,0:T(8,128)(2,1)}, f32[6,2,3072]{2...) while((s32[]{:T(128)}, bf16[6,512,128]{1,2,0:T(8,128)(2,1)}, ...), condition=%wide.region_47.48_spmd.clone, body=%wide.region_29.47_spmd.clone.sunk | while | flops 1373513728 | bytes 225066688 | solution.py:397
  1588.6 12.8 fusion.61
  1601.4 10.6 fusion.58
  1627.8 37.1 %reduce-scatter.5.cloned.1.call-done = bf16[512,768]{0,1:T(8,128)(2,1)} async-done(((bf16[2048,768]{0,1:T(8,128)(2,1)}), bf16[512,768]{0,1:T(8,128)(2,1)}) %reduce-scatter.5.cloned.1.call-update) | async-done | bytes 786448 | tf_op jit(solution)/shard_map/reduce_scatter | solution.py:401
  1679.4 42.7 %reduce-scatter.11.cloned.1.call-done = bf16[1,384,768]{2,1,0:T(8,128)(2,1)} async-done(((bf16[1,3072,768]{2,1,0:T(8,128)(2,1)}), bf16[1,384,768]{2,1,0:T(8,128)(2,1)}) %reduce-scatter.11.cloned.1.call-update) | async-done | bytes 589840 | tf_op jit(solution)/shard_map/reduce_scatter | solution.py:445
  1724.3 55.4 %reduce-scatter.9.cloned.1.call-done = bf16[1,96,3072]{2,1,0:T(8,128)(2,1)} async-done(((bf16[1,768,3072]{2,1,0:T(8,128)(2,1)}), bf16[1,96,3072]{2,1,0:T(8,128)(2,1)}) %reduce-scatter.9.cloned.1.call-update) | async-done | bytes 589840 | tf_op jit(solution)/shard_map/reduce_scatter | solution.py:442
  1787.4 42.3 %all-reduce.54 = (f32[768]{0:T(1024)}, f32[32,12]{0,1:T(8,128)}, f32[768]{0:T(1024)}, f32[768,4]{0,1:T(4,128)}) all-reduce(f32[768]{0:T(1024)} %get-tuple-element.1217, f32[32,12]{0,1:T(8,128)} %fusion.87, f32[768]{0:T(1024)} %get-tuple-element.1213, ...), channel_id=1, replica_groups=mesh['dp'=2,'context'=4,'expert'=4] {'dp','context','expert'}, use_global_device_ids=true, to_apply=%region_52.53 | all-reduce | flops 4992 | bytes 39936 | tf_op jit(solution)/shard_map/psum | solution.py:428
  1833.5 146.6 %all-reduce.58.cloned.1.call-done = (f32[768,768]{1,0:T(8,128)}, f32[768,768]{1,0:T(8,128)}, f32[768,768]{1,0:T(8,128)}, f32[768,768]{1,0:T(8,128)}) async-done(((f32[768,768]{1,0:T(8,128)}, f32[768,768]{1,0:T(8,128)}, f32[768,768]{1,0:T(8,128)}, f32[768,768]{1,0:T(8,128)}), (f32[768,768]{1,0:T(8,128)}, f32[768,768]{1,0:T(8,128)}, f32[768,768]{1,0:T(8,128)}, ...) | async-done | bytes 9437200 | tf_op jit(solution)/shard_map/psum | solution.py:428
  (1844 shorter events, 1223.0 us)
Async XLA Ops:
  7.2 592.7 %all-gather.3.cloned.1.call-start = ((), (), s32[]{:S(2)}) async-start(), calls=%async_computation.8 | async-start | bytes 3932160 | tf_op jit(solution)/shard_map/all_gather | solution.py:236
  12.3 11.1 copy-start.100
  12.3 592.4 %all-gather.5.cloned.1.call-start = ((), (), s32[]{:S(2)}) async-start(), calls=%async_computation.9 | async-start | bytes 3932160 | tf_op jit(solution)/shard_map/all_gather | solution.py:235
  135.5 11.3 copy-start.104
  395.6 31.8 %copy-start.71 = (f32[12,383]{1,0:T(8,128)S(1)}, f32[12,383]{1,0:T(8,128)}, u32[]{:S(2)}) copy-start(f32[12,383]{1,0:T(8,128)} %get-tuple-element.1379) | copy-start | bytes 55156
  465.8 20.1 %copy-start.70 = (f32[12,383]{1,0:T(8,128)S(1)}, f32[12,383]{1,0:T(8,128)}, u32[]{:S(2)}) copy-start(f32[12,383]{1,0:T(8,128)} %get-tuple-element.1380) | copy-start | bytes 55156
  609.5 74.1 %copy-start.26 = (bf16[1,2,128,768]{3,2,1,0:T(8,128)(2,1)S(1)}, bf16[1,2,128,768]{3,2,1,0:T(8,128)(2,1)}, u32[]{:S(2)}) copy-start(bf16[1,2,128,768]{3,2,1,0:T(8,128)(2,1)} %param.95) | copy-start | bytes 1179652
  609.6 74.1 %copy-start.31 = (bf16[1,256,768]{2,1,0:T(8,128)(2,1)S(1)}, bf16[1,256,768]{2,1,0:T(8,128)(2,1)}, u32[]{:S(2)}) copy-start(bf16[1,256,768]{2,1,0:T(8,128)(2,1)} %param.94) | copy-start | bytes 1179652
  687.5 20.7 %copy-start.19 = (bf16[512,768]{1,0:T(8,128)(2,1)}, bf16[512,768]{1,0:T(8,128)(2,1)S(1)}, u32[]{:S(2)}) copy-start(bf16[512,768]{1,0:T(8,128)(2,1)S(1)} %multiply_convert_fusion.1) | copy-start | bytes 2359300
  692.6 47.7 %all-to-all-start = ((bf16[4,288,768]{2,1,0:T(8,128)(2,1)}), bf16[4,288,768]{2,1,0:T(8,128)(2,1)}, u32[]{:S(2)}, u32[]{:S(2)}) async-start(bf16[4,288,768]{2,1,0:T(8,128)(2,1)} %bitcast.667), calls=%async_computation | async-start | bytes 3538944 | tf_op jit(solution)/shard_map/all_to_all | solution.py:278
  740.3 44.2 %all-to-all-start.2 = ((bf16[4,288,768]{2,1,0:T(8,128)(2,1)}), bf16[4,288,768]{2,1,0:T(8,128)(2,1)S(1)}, u32[]{:S(2)}, u32[]{:S(2)}) async-start(bf16[4,288,768]{2,1,0:T(8,128)(2,1)} %bitcast.668), calls=%async_computation.2 | async-start | bytes 3538944 | tf_op jit(solution)/shard_map/all_to_all | solution.py:310
  785.7 44.6 %all-to-all-start.1 = ((bf16[4,288,768]{2,1,0:T(8,128)(2,1)}), bf16[4,288,768]{2,1,0:T(8,128)(2,1)S(1)}, u32[]{:S(2)}, u32[]{:S(2)}) async-start(bf16[4,288,768]{2,1,0:T(8,128)(2,1)} %fusion.70), calls=%async_computation.1 | async-start | bytes 3538944 | tf_op jit(solution)/shard_map/all_to_all | solution.py:286
  818.9 15.9 copy-start.78
  818.9 15.9 copy-start.80
  830.3 12.7 copy-start.22
  830.3 45.2 %all-to-all-start.3 = ((bf16[4,288,768]{2,1,0:T(8,128)(2,1)}), bf16[4,288,768]{2,1,0:T(8,128)(2,1)}, u32[]{:S(2)}, u32[]{:S(2)}) async-start(bf16[4,288,768]{2,1,0:T(8,128)(2,1)} %fusion.75), calls=%async_computation.3 | async-start | bytes 3538944 | tf_op jit(solution)/shard_map/all_to_all | solution.py:327
  834.8 789.6 %reduce-scatter.7.cloned.1.call-start = ((), (), s32[]{:S(2)}) async-start(), calls=%async_computation.11 | async-start | bytes 3932160 | tf_op jit(solution)/shard_map/reduce_scatter | solution.py:407
  867.9 26.4 %copy-start.47 = (f32[512,1,4]{2,1,0:T(1,128)}, f32[512,1,4]{2,1,0:T(1,128)S(1)}, u32[]{:S(2)}) copy-start(f32[512,1,4]{2,1,0:T(1,128)S(1)} %fusion.88) | copy-start | bytes 24580
  997.9 9.5 copy-start.4
  1000.6 14.3 copy-start.3
  1110.0 14.3 copy-start.3
  1219.5 14.3 copy-start.3
  1328.9 14.3 copy-start.3
  1438.3 14.3 copy-start.3
  1547.8 14.3 copy-start.3
  1587.2 77.7 %reduce-scatter.5.cloned.1.call-start = ((), (), s32[]{:S(2)}) async-start(), calls=%async_computation.10 | async-start | bytes 3932160 | tf_op jit(solution)/shard_map/reduce_scatter | solution.py:401
  1587.7 134.4 %reduce-scatter.11.cloned.1.call-start = ((), (), s32[]{:S(2)}) async-start(), calls=%async_computation.13 | async-start | bytes 5308416 | tf_op jit(solution)/shard_map/reduce_scatter | solution.py:445
  1601.4 178.3 %reduce-scatter.9.cloned.1.call-start = ((), (), s32[]{:S(2)}) async-start(), calls=%async_computation.12 | async-start | bytes 5308416 | tf_op jit(solution)/shard_map/reduce_scatter | solution.py:442
  1612.1 368.0 %all-reduce.58.cloned.1.call-start = ((), (), s32[]{:S(2)}) async-start(), calls=%async_computation.14 | async-start | bytes 18874368 | tf_op jit(solution)/shard_map/psum | solution.py:428
  1724.3 60.1 %copy-start.28 = (bf16[1,2,128,768]{3,2,1,0:T(8,128)(2,1)S(1)}, bf16[1,2,128,768]{3,2,1,0:T(8,128)(2,1)}, u32[]{:S(2)}) copy-start(bf16[1,2,128,768]{3,2,1,0:T(8,128)(2,1)} %param.95) | copy-start | bytes 1179652
  1724.3 60.1 %copy-start.33 = (bf16[1,256,768]{2,1,0:T(8,128)(2,1)S(1)}, bf16[1,256,768]{2,1,0:T(8,128)(2,1)}, u32[]{:S(2)}) copy-start(bf16[1,256,768]{2,1,0:T(8,128)(2,1)} %param.94) | copy-start | bytes 1179652
  1784.4 45.3 %copy-start.89 = (f32[512]{0:T(512)S(1)}, f32[512]{0:T(512)}, u32[]{:S(2)}) copy-start(f32[512]{0:T(512)} %copy-done.88) | copy-start | bytes 6148
  (186 other events, 1038.0 us)
Sparse Core Ops, SparseCore 0:
  12.4 31.2 all-gather.2
  45.8 28.6 all-gather.4
  1587.3 36.9 reduce-scatter.6
  1626.9 37.9 reduce-scatter.4
  1668.2 53.8 reduce-scatter.10
  1725.8 53.8 reduce-scatter.8
  1787.1 192.9 all-reduce.57
where the time goes:
time: 2020 us; the launch traced here: 2000 us
  local copies, waits for them, and re-layouts  1040 us (51%)
  waiting for transfers between devices  343 us (17%)
  matrix products  255 us (13%)
  other arithmetic  248 us (12%)
  blocking collectives  42.3 us (2%)
  loops' own time  31.7 us (2%)
    scatter x36, local copies, waits for them, and re-layouts, build_bias(): result = result.at[:, q_off:q_off + q_len, k_off:k_off + k_len].set(tile)  276 us
    psum x1, waiting for transfers between devices, body(): lax.psum((attn_gain_grad, query_grad, key_grad, value_grad, attn_out_grad...  147 us
    reshape x96, local copies, waits for them, and re-layouts, diagonal_sums(): flat = padded.reshape(heads, rows * (width - 1))  113 us
    reshape x16, local copies, waits for them, and re-layouts, toeplitz_tile(): return flat.reshape(heads, rows, width - 1)[:, :, :cols]  108 us
    unnamed x275, local copies, waits for them, and re-layouts  86.7 us
    while x330, local copies, waits for them, and re-layouts  83.3 us
    dynamic_update_slice x96, local copies, waits for them, and re-layouts, distance_grad(): total = lax.dynamic_update_slice_in_dim(total, current + sums, begin, 1)  69.7 us
    dot_general x12, matrix products, pair_scores(): jnp.einsum('qhd,khd->hqk', two_heads(query_pair), two_heads(key_pair), pr...  66.1 us
  transfers between devices with their start and end apart: 11, of which 9 were waited for; matrix products, arithmetic and copies ran while one was open for 38% of the time, Pallas kernels for 0%

commit v1 on v0

v1 whole, which is shorter than its diff:
```python
import functools

import jax
import jax.numpy as jnp
from jax import lax
from jax.experimental import pallas as pl
from jax.experimental.pallas import tpu as pltpu
from jax.sharding import PartitionSpec as P

HD = 64
BK = 256
EPSILON = 1e-06
MASKED = -1e30
F32 = jnp.float32
BF16 = jnp.bfloat16
PRECISE = lax.Precision.HIGHEST
VMEM = pltpu.VMEM
MIB = 1 << 20


def dot(a, b):
    return lax.dot_general(a, b, (((1,), (0,)), ((), ())), preferred_element_type=F32)


def dot_nt(a, b):
    return lax.dot_general(a, b, (((1,), (1,)), ((), ())), preferred_element_type=F32)


def dot_tn(a, b):
    return lax.dot_general(a, b, (((0,), (0,)), ((), ())), preferred_element_type=F32)


def split_dot(a, b, op):
    high = a.astype(BF16)
    low = (a - high.astype(F32)).astype(BF16)
    return op(high, b) + op(low, b)


def full(shape):
    return pl.BlockSpec(shape, lambda *_: (0,) * len(shape))


class Layout:
    def __init__(self, spread, prompt_rows, cont_count, cont_rows):
        assert prompt_rows == BK and BK % cont_rows == 0
        self.spread = spread
        self.prompt_rows = prompt_rows
        self.cont_count = cont_count
        self.cont_rows = cont_rows
        self.tokens = prompt_rows + cont_count * cont_rows
        self.per_cont = spread * cont_rows // BK
        self.blocks = spread + cont_count * self.per_cont
        self.total = self.blocks * BK
        self.keys, self.place, self.pieces = [], [], []
        for p in range(spread):
            self.keys.append(list(range(p + 1)))
            self.place.append(p)
            self.pieces.append([(p, 0, 0, BK)])
        each = BK // cont_rows
        for j in range(cont_count):
            for m in range(self.per_cont):
                first = spread + j * self.per_cont
                self.keys.append(list(range(spread)) + list(range(first, first + m + 1)))
                self.place.append(spread + m)
                self.pieces.append(
                    [
                        (m * each + n, prompt_rows + j * cont_rows, n * cont_rows, cont_rows)
                        for n in range(each)
                    ]
                )
        self.tile = {}
        for q in range(self.blocks):
            for k in self.keys[q]:
                self.tile[(q, k)] = len(self.tile)
        self.tiles = len(self.tile)
        self.distances = spread + self.per_cont

    def distance(self, q, k):
        return self.place[q] - self.place[k]


def plan_kernel(
    experts, capacity, route_ref, route_t_ref, order_row_ref, order_col_ref, dz_ref, rows_ref, cols_ref, dzp_ref
):
    tokens = dz_ref.shape[0]
    slots = experts * capacity
    side = (tokens, tokens)
    lane = lax.broadcasted_iota(jnp.int32, side, 1)
    sub = lax.broadcasted_iota(jnp.int32, side, 0)
    rank_col = jnp.sum(
        jnp.where(order_row_ref[...] == sub, lane, 0).astype(F32), axis=1, keepdims=True
    )
    rank_row = jnp.sum(
        jnp.where(order_col_ref[...] == lane, sub, 0).astype(F32), axis=0, keepdims=True
    )
    before = jnp.where(rank_row < rank_col, 1.0, 0.0).astype(BF16)
    before_t = jnp.where(rank_col < rank_row, 1.0, 0.0).astype(BF16)
    expert_lane = lax.broadcasted_iota(jnp.int32, (tokens, 128), 1)
    hots = [jnp.where(route_ref[:, i : i + 1] == expert_lane, 1.0, 0.0) for i in range(2)]
    counts = [dot(before, hot.astype(BF16)) for hot in hots]
    counts[1] = counts[1] + jnp.sum(hots[0], axis=0, keepdims=True)
    expert_sub = lax.broadcasted_iota(jnp.int32, (16, tokens), 0)
    hots_t = [jnp.where(route_t_ref[i : i + 1, :] == expert_sub, 1.0, 0.0) for i in range(2)]
    counts_t = [dot(hot.astype(BF16), before_t) for hot in hots_t]
    counts_t[1] = counts_t[1] + jnp.sum(hots_t[0], axis=1, keepdims=True)
    slot_rows = []
    cols = jnp.full((tokens, 128), -1, jnp.int32)
    for i in range(2):
        pos = jnp.sum(hots[i] * counts[i], axis=1, keepdims=True).astype(jnp.int32)
        slot = jnp.where(pos < capacity, route_ref[:, i : i + 1] * capacity + pos, -1)
        cols = jnp.where(expert_lane == i, slot, cols)
        pos = jnp.sum(hots_t[i] * counts_t[i], axis=0, keepdims=True).astype(jnp.int32)
        slot_rows.append(jnp.where(pos < capacity, route_t_ref[i : i + 1, :] * capacity + pos, -1))
    cols_ref[...] = cols
    sub8 = lax.broadcasted_iota(jnp.int32, (8, tokens), 0)
    rows_ref[...] = jnp.where(sub8 == 0, slot_rows[0], jnp.where(sub8 == 1, slot_rows[1], -1))
    dz = dz_ref[...]
    for start in range(0, slots, 128):
        number = lax.broadcasted_iota(jnp.int32, (128, tokens), 0) + start
        first = jnp.where(slot_rows[0] == number, 1.0, 0.0)
        second = jnp.where(slot_rows[1] == number, 1.0, 0.0)
        dzp_ref[start : start + 128, : dz.shape[1]] = dot((first + second).astype(BF16), dz).astype(BF16)
        other = dot(first.astype(BF16), hots[1].astype(BF16)) + dot(
            second.astype(BF16), hots[0].astype(BF16)
        )
        dzp_ref[start : start + 128, dz.shape[1] :] = other.astype(BF16)


def plan(routes, ranking, upstream, experts, capacity):
    tokens, width = upstream.shape
    return pl.pallas_call(
        functools.partial(plan_kernel, experts, capacity),
        out_shape=(
            jax.ShapeDtypeStruct((8, tokens), jnp.int32),
            jax.ShapeDtypeStruct((tokens, 128), jnp.int32),
            jax.ShapeDtypeStruct((experts * capacity, width + 128), BF16),
        ),
        compiler_params=pltpu.CompilerParams(vmem_limit_bytes=32 * MIB),
        name="slot_plan",
    )(routes, routes.T, ranking.reshape(1, tokens), ranking.reshape(tokens, 1), upstream)


def toeplitz_tile(table_row, d):
    line = jnp.concatenate(
        [table_row[:, (d + 1) * BK : (d + 2) * BK], table_row[:, d * BK : (d + 1) * BK]], axis=1
    )
    tile = jnp.broadcast_to(line, (8, 2 * BK))
    row = lax.broadcasted_iota(jnp.int32, (8, 2 * BK), 0)
    for bit in (1, 2, 4):
        tile = jnp.where((row & bit) > 0, pltpu.roll(tile, bit, 1), tile)
    height = 8
    while height < BK:
        tile = jnp.concatenate([tile, pltpu.roll(tile, height, 1)], axis=0)
        height *= 2
    tile = tile[:, :BK]
    if d == 0:
        key = lax.broadcasted_iota(jnp.int32, (BK, BK), 0)
        query = lax.broadcasted_iota(jnp.int32, (BK, BK), 1)
        tile = jnp.where(query >= key, tile, MASKED)
    return tile


def diagonal_sums(tile):
    tile = jnp.concatenate([tile, jnp.zeros((BK, BK), F32)], axis=1)
    height = BK
    while height > 8:
        height //= 2
        tile = tile[:height] + pltpu.roll(tile[height:], 2 * BK - height, 1)
    row = lax.broadcasted_iota(jnp.int32, (8, 2 * BK), 0)
    for bit in (1, 2, 4):
        tile = jnp.where((row & bit) > 0, pltpu.roll(tile, 2 * BK - bit, 1), tile)
    return jnp.sum(tile, axis=0, keepdims=True)


def attention_kernel(
    lay, heads, x_ref, gain_ref, w_ref, tab_ref, h1_ref, qkvn_ref, qkvt_ref, e_ref, ot_ref, rl_ref, at_ref, s_scr, bias_scr
):
    h = pl.program_id(0)

    @pl.when(h == 0)
    def _():
        for block in range(lay.blocks):
            base = block * BK
            for c, start, at, size in lay.pieces[block]:
                x = x_ref[c, start : start + size].astype(F32)
                r = lax.rsqrt(jnp.mean(x * x, axis=1, keepdims=True) + EPSILON)
                h1_ref[base + at : base + at + size] = (x * r * gain_ref[...]).astype(BF16)
            y = dot(h1_ref[base : base + BK], w_ref[...]).astype(BF16)
            scale = jnp.where(lax.broadcasted_iota(jnp.int32, y.shape, 1) < heads * HD, HD**-0.5, 1.0)
            y = (y.astype(F32) * scale).astype(BF16)
            yt = y.T
            qkvt_ref[:, base : base + BK] = yt
            for i in range(3 * heads):
                qkvn_ref[i, base : base + BK] = y[:, i * HD : (i + 1) * HD]

    table_row = tab_ref[0]
    for d in range(lay.distances):
        bias_scr[d] = toeplitz_tile(table_row, d)
    hrow = pl.multiple_of(h * HD, HD)
    for q in range(lay.blocks):
        qt = qkvt_ref[pl.ds(hrow, HD), q * BK : (q + 1) * BK]
        top = None
        for n, k in enumerate(lay.keys[q]):
            s = dot(qkvn_ref[heads + h, k * BK : (k + 1) * BK], qt) + bias_scr[lay.distance(q, k)]
            s_scr[n] = s
            m = jnp.max(s, axis=0, keepdims=True)
            top = m if top is None else jnp.maximum(top, m)
        total, out = 0.0, 0.0
        vrow = pl.multiple_of(2 * heads * HD + h * HD, HD)
        for n, k in enumerate(lay.keys[q]):
            e = jnp.exp(s_scr[n] - top)
            total = total + jnp.sum(e, axis=0, keepdims=True)
            e = e.astype(BF16)
            e_ref[0, lay.tile[(q, k)]] = e
            out = out + dot(qkvt_ref[pl.ds(vrow, HD), k * BK : (k + 1) * BK], e)
        inverse = 1.0 / total
        rl_ref[0, :, q * BK : (q + 1) * BK] = inverse
        out = out * inverse
        ot_ref[pl.ds(hrow, HD), q * BK : (q + 1) * BK] = out
        for c, start, at, size in lay.pieces[q]:
            at_ref[c, pl.ds(hrow, HD), start : start + size] = out[:, at : at + size].astype(BF16)


def attention_forward(lay, heads, x_all, gain, weights, table):
    width = x_all.shape[2]
    feats = heads * HD
    return pl.pallas_call(
        functools.partial(attention_kernel, lay, heads),
        grid=(heads,),
        in_specs=[
            full(x_all.shape),
            full((1, width)),
            full(weights.shape),
            pl.BlockSpec((1, 1, table.shape[2]), lambda h: (h, 0, 0)),
        ],
        out_specs=(
            full((lay.total, width)),
            full((3 * heads, lay.total, HD)),
            full((3 * feats, lay.total)),
            pl.BlockSpec((1, lay.tiles, BK, BK), lambda h: (h, 0, 0, 0)),
            full((feats, lay.total)),
            pl.BlockSpec((1, 1, lay.total), lambda h: (h, 0, 0)),
            full((lay.spread, feats, lay.tokens)),
        ),
        out_shape=(
            jax.ShapeDtypeStruct((lay.total, width), BF16),
            jax.ShapeDtypeStruct((3 * heads, lay.total, HD), BF16),
            jax.ShapeDtypeStruct((3 * feats, lay.total), BF16),
            jax.ShapeDtypeStruct((heads, lay.tiles, BK, BK), BF16),
            jax.ShapeDtypeStruct((feats, lay.total), F32),
            jax.ShapeDtypeStruct((heads, 1, lay.total), F32),
            jax.ShapeDtypeStruct((lay.spread, feats, lay.tokens), BF16),
        ),
        scratch_shapes=[
            VMEM((max(len(k) for k in lay.keys), BK, BK), F32),
            VMEM((lay.distances, BK, BK), F32),
        ],
        compiler_params=pltpu.CompilerParams(vmem_limit_bytes=58 * MIB),
        name="attention_forward",
    )(x_all, gain, weights, table)


def middle_kernel(
    experts, capacity, at_ref, x_ref, wo_ref, gain_ref, router_ref, route_ref, rows_ref, mid_ref, h2_ref, gates_ref, sent_ref
):
    mid = x_ref[...].astype(F32) + dot_tn(at_ref[...], wo_ref[...])
    mid_ref[...] = mid
    r = lax.rsqrt(jnp.mean(mid * mid, axis=1, keepdims=True) + EPSILON)
    h2 = (mid * r * gain_ref[...]).astype(BF16)
    h2_ref[...] = h2
    tokens = h2.shape[0]
    for start in range(0, experts * capacity, 128):
        number = lax.broadcasted_iota(jnp.int32, (128, tokens), 0) + start
        pick = (rows_ref[0:1, :] == number) | (rows_ref[1:2, :] == number)
        pick = jnp.where(pick, 1.0, 0.0).astype(BF16)
        sent_ref[start : start + 128] = dot(pick, h2).astype(BF16)
    logits = dot(h2, router_ref[...])
    lane = lax.broadcasted_iota(jnp.int32, logits.shape, 1)
    chosen = [
        jnp.sum(jnp.where(route_ref[:, i : i + 1] == lane, logits, 0.0), axis=1, keepdims=True)
        for i in range(2)
    ]
    most = jnp.maximum(chosen[0], chosen[1])
    parts = [jnp.exp(c - most) for c in chosen]
    inverse = 1.0 / (parts[0] + parts[1])
    wide = lax.broadcasted_iota(jnp.int32, (tokens, 128), 1)
    gates_ref[...] = jnp.where(
        wide == 0, parts[0] * inverse, jnp.where(wide == 1, parts[1] * inverse, 0.0)
    )


def middle(attended_t, x_local, w_attn_out, gain, router, routes, rows, experts, capacity):
    tokens, width = x_local.shape
    return pl.pallas_call(
        functools.partial(middle_kernel, experts, capacity),
        out_shape=(
            jax.ShapeDtypeStruct((tokens, width), F32),
            jax.ShapeDtypeStruct((tokens, width), BF16),
            jax.ShapeDtypeStruct((tokens, 128), F32),
            jax.ShapeDtypeStruct((experts * capacity, width), BF16),
        ),
        compiler_params=pltpu.CompilerParams(vmem_limit_bytes=40 * MIB),
        name="middle",
    )(attended_t, x_local, w_attn_out, gain, router, routes, rows)


def gelu_parts(u):
    slope = 0.7978845608028654
    cube = 0.044715
    square = u * u
    t = jnp.tanh(slope * u * (1.0 + cube * square))
    half = 0.5 * (1.0 + t)
    value = u * half
    grad = half + 0.5 * u * (1.0 - t * t) * (slope * (1.0 + 3.0 * cube * square))
    return value, grad


def expert_grad_kernel(
    steps, sent_ref, dzp_ref, router_ref, w_in_ref, w_out_ref, act_ref, dpre_ref, dsent_ref, dmade_ref, share_ref, acc, shares
):
    f = pl.program_id(0)
    width = sent_ref.shape[1]

    @pl.when(f == 0)
    def _():
        logits = dot(sent_ref[...], router_ref[...])
        lane = lax.broadcasted_iota(jnp.int32, logits.shape, 1)
        own = jnp.sum(
            jnp.where(lane == lax.axis_index("expert"), logits, 0.0), axis=1, keepdims=True
        )
        other_hot = dzp_ref[:, width : width + logits.shape[1]].astype(F32)
        other = jnp.sum(other_hot * logits, axis=1, keepdims=True)
        gate = 1.0 / (1.0 + jnp.exp(other - own))
        dmade_ref[...] = (gate * dzp_ref[:, :width].astype(F32)).astype(BF16)
        acc[...] = jnp.zeros_like(acc)
        shares[...] = jnp.zeros_like(shares)

    pre = dot(sent_ref[...], w_in_ref[0])
    dact = dot_nt(dmade_ref[...], w_out_ref[0])
    value, grad = gelu_parts(pre)
    act = value.astype(BF16)
    act_ref[...] = act
    dpre = (dact * grad).astype(BF16)
    dpre_ref[...] = dpre
    product = act.astype(F32) * dact
    part = product[:, :128]
    for i in range(1, product.shape[1] // 128):
        part = part + product[:, i * 128 : (i + 1) * 128]
    shares[...] += part
    acc[...] += dot_nt(dpre, w_in_ref[0])

    @pl.when(f == steps - 1)
    def _():
        dsent_ref[...] = acc[...].astype(BF16)
        total = jnp.sum(shares[...], axis=1, keepdims=True)
        share_ref[...] = jnp.broadcast_to(total, share_ref.shape)


def expert_grad(sent, dzp, router, w_in, w_out):
    rows, width = sent.shape
    hidden = w_in.shape[2]
    chunk = 512
    steps = hidden // chunk
    return pl.pallas_call(
        functools.partial(expert_grad_kernel, steps),
        grid=(steps,),
        in_specs=[
            full((rows, width)),
            full(dzp.shape),
            full(router.shape),
            pl.BlockSpec((1, width, chunk), lambda f: (0, 0, f)),
            pl.BlockSpec((1, chunk, width), lambda f: (0, f, 0)),
        ],
        out_specs=(
            pl.BlockSpec((rows, chunk), lambda f: (0, f)),
            pl.BlockSpec((rows, chunk), lambda f: (0, f)),
            full((rows, width)),
            full((rows, width)),
            full((rows, 128)),
        ),
        out_shape=(
            jax.ShapeDtypeStruct((rows, hidden), BF16),
            jax.ShapeDtypeStruct((rows, hidden), BF16),
            jax.ShapeDtypeStruct((rows, width), BF16),
            jax.ShapeDtypeStruct((rows, width), BF16),
            jax.ShapeDtypeStruct((rows, 128), F32),
        ),
        scratch_shapes=[VMEM((rows, width), F32), VMEM((rows, 128), F32)],
        compiler_params=pltpu.CompilerParams(vmem_limit_bytes=56 * MIB),
        name="expert_grad",
    )(sent, dzp, router, w_in, w_out)


def expert_weight_kernel(
    steps, sent_ref, dmade_ref, act_ref, dpre_ref, w_out_ref, made_ref, gin_ref, gout_ref, acc
):
    f = pl.program_id(0)

    @pl.when(f == 0)
    def _():
        acc[...] = jnp.zeros_like(acc)

    acc[...] += dot(act_ref[...], w_out_ref[0])
    gout_ref[0] = dot_tn(act_ref[...], dmade_ref[...]).astype(BF16)
    gin_ref[0] = dot_tn(sent_ref[...], dpre_ref[...]).astype(BF16)

    @pl.when(f == steps - 1)
    def _():
        made_ref[...] = acc[...].astype(BF16)


def expert_weights(sent, dmade, act, dpre, w_out):
    rows, width = sent.shape
    hidden = act.shape[1]
    chunk = 512
    steps = hidden // chunk
    return pl.pallas_call(
        functools.partial(expert_weight_kernel, steps),
        grid=(steps,),
        in_specs=[
            full((rows, width)),
            full((rows, width)),
            pl.BlockSpec((rows, chunk), lambda f: (0, f)),
            pl.BlockSpec((rows, chunk), lambda f: (0, f)),
            pl.BlockSpec((1, chunk, width), lambda f: (0, f, 0)),
        ],
        out_specs=(
            full((rows, width)),
            pl.BlockSpec((1, width, chunk), lambda f: (0, 0, f)),
            pl.BlockSpec((1, chunk, width), lambda f: (0, f, 0)),
        ),
        out_shape=(
            jax.ShapeDtypeStruct((rows, width), BF16),
            jax.ShapeDtypeStruct((1, width, hidden), BF16),
            jax.ShapeDtypeStruct((1, hidden, width), BF16),
        ),
        scratch_shapes=[VMEM((rows, width), F32)],
        compiler_params=pltpu.CompilerParams(vmem_limit_bytes=56 * MIB),
        name="expert_weights",
    )(sent, dmade, act, dpre, w_out)


def turn_kernel(
    slots, dsent_ref, share_ref, cols_ref, gates_ref, route_ref, mid_ref, dz_ref, h2_ref, gain_ref, router_ref, wo_ref, at_ref, dmid_ref, dot_ref, gwo_ref, ggain_ref, grouter_ref
):
    tokens = mid_ref.shape[0]
    lane = lax.broadcasted_iota(jnp.int32, (tokens, slots), 1)
    picks = [cols_ref[:, i : i + 1] == lane for i in range(2)]
    both = jnp.where(picks[0] | picks[1], 1.0, 0.0).astype(BF16)
    dh2 = dot(both, dsent_ref[...])
    share = [
        jnp.sum(jnp.where(picks[i], share_ref[0:1, :], 0.0), axis=1, keepdims=True)
        for i in range(2)
    ]
    total = share[0] + share[1]
    dchosen = [share[i] - gates_ref[:, i : i + 1] * total for i in range(2)]
    experts = router_ref.shape[1]
    elane = lax.broadcasted_iota(jnp.int32, (tokens, experts), 1)
    dlogits = sum(
        jnp.where(route_ref[:, i : i + 1] == elane, dchosen[i], 0.0) for i in range(2)
    )
    dh2 = dh2 + split_dot(dlogits, router_ref[...], dot_nt)
    grouter_ref[...] = split_dot(dlogits, h2_ref[...], dot_tn)
    mid = mid_ref[...]
    r = lax.rsqrt(jnp.mean(mid * mid, axis=1, keepdims=True) + EPSILON)
    u = dh2 * gain_ref[...]
    mean = jnp.mean(u * mid, axis=1, keepdims=True)
    dmid = dz_ref[...].astype(F32) + r * u - (r * r * r) * mid * mean
    dmid_ref[...] = dmid
    ggain_ref[...] = jnp.sum(dh2 * mid * r, axis=0, keepdims=True)
    branch = dmid.astype(BF16)
    gwo_ref[...] = dot(at_ref[...], branch)
    dot_ref[...] = dot_nt(wo_ref[...], branch).astype(BF16)


def turn(dsent, share, cols, gates, routes, mid, dz, h2, gain, router, wo, attended_t):
    tokens, width = mid.shape
    return pl.pallas_call(
        functools.partial(turn_kernel, dsent.shape[0]),
        out_shape=(
            jax.ShapeDtypeStruct((tokens, width), F32),
            jax.ShapeDtypeStruct((width, tokens), BF16),
            jax.ShapeDtypeStruct((width, width), F32),
            jax.ShapeDtypeStruct((1, width), F32),
            jax.ShapeDtypeStruct((router.shape[1], width), F32),
        ),
        compiler_params=pltpu.CompilerParams(vmem_limit_bytes=48 * MIB),
        name="turn",
    )(dsent, share, cols, gates, routes, mid, dz, h2, gain, router, wo, attended_t)


def attention_back_kernel(
    lay, heads, dot_ref, e_ref, qkvn_ref, qkvt_ref, ot_ref, rl_ref, h1_ref, wt_ref, dh1_ref, gw_ref, gtab_ref, dst_scr, doT_scr, do_scr, dT_scr
):
    h = pl.program_id(0)
    feats = heads * HD
    hrow = pl.multiple_of(h * HD, HD)
    deltas = []
    for q in range(lay.blocks):
        cols = slice(q * BK, (q + 1) * BK)
        for c, start, at, size in lay.pieces[q]:
            piece = dot_ref[c, pl.ds(hrow, HD), start : start + size]
            where = q * BK + at
            doT_scr[:, where : where + size] = piece
        raw = doT_scr[:, cols].astype(F32)
        inverse = rl_ref[0, :, cols]
        deltas.append(
            inverse * jnp.sum(raw * ot_ref[pl.ds(hrow, HD), cols], axis=0, keepdims=True)
        )
        scaled = raw * inverse
        doT_scr[:, cols] = scaled.astype(BF16)
        do_scr[cols] = scaled.T.astype(BF16)
    krow = pl.multiple_of(feats + h * HD, HD)
    vrow = pl.multiple_of(2 * feats + h * HD, HD)
    for q in range(lay.blocks):
        cols = slice(q * BK, (q + 1) * BK)
        dq = 0.0
        for k in lay.keys[q]:
            t = lay.tile[(q, k)]
            rows = slice(k * BK, (k + 1) * BK)
            dp = dot(qkvn_ref[2 * heads + h, rows], doT_scr[:, cols])
            ds = (e_ref[0, t].astype(F32) * (dp - deltas[q])).astype(BF16)
            dst_scr[t] = ds
            dq = dq + dot(qkvt_ref[pl.ds(krow, HD), rows], ds)
        dT_scr[pl.ds(hrow, HD), cols] = (dq * HD**-0.5).astype(BF16)
    for k in range(lay.blocks):
        rows = slice(k * BK, (k + 1) * BK)
        dk, dv = 0.0, 0.0
        for q in range(lay.blocks):
            if k in lay.keys[q]:
                t = lay.tile[(q, k)]
                cols = slice(q * BK, (q + 1) * BK)
                dk = dk + dot(dst_scr[t], qkvn_ref[h, cols])
                dv = dv + dot(e_ref[0, t], do_scr[cols])
        dT_scr[pl.ds(krow, HD), rows] = dk.T.astype(BF16)
        dT_scr[pl.ds(vrow, HD), rows] = dv.T.astype(BF16)
    gtab_ref[...] = jnp.zeros_like(gtab_ref)
    for d in range(lay.distances):
        tile = 0.0
        for (q, k), t in lay.tile.items():
            if lay.distance(q, k) == d:
                tile = tile + dst_scr[t].astype(F32)
        sums = diagonal_sums(tile)
        gtab_ref[0, :, (d + 1) * BK : (d + 2) * BK] += sums[:, :BK]
        gtab_ref[0, :, d * BK : (d + 1) * BK] += sums[:, BK:]

    @pl.when(h == heads - 1)
    def _():
        for q in range(lay.blocks):
            cols = slice(q * BK, (q + 1) * BK)
            part = dot_tn(dT_scr[:, cols], wt_ref[...]).astype(BF16)
            for c, start, at, size in lay.pieces[q]:
                dh1_ref[c, start : start + size] = part[at : at + size]
        gw_ref[...] = dot(dT_scr[...], h1_ref[...])


def attention_backward(lay, heads, dattn_t, e, qkvn, qkvt, ot, rl, h1, weights_t):
    width = h1.shape[1]
    feats = heads * HD
    span = (lay.distances + 1) * BK
    return pl.pallas_call(
        functools.partial(attention_back_kernel, lay, heads),
        grid=(heads,),
        in_specs=[
            full(dattn_t.shape),
            pl.BlockSpec((1, lay.tiles, BK, BK), lambda h: (h, 0, 0, 0)),
            full(qkvn.shape),
            full(qkvt.shape),
            full(ot.shape),
            pl.BlockSpec((1, 1, lay.total), lambda h: (h, 0, 0)),
            full(h1.shape),
            full(weights_t.shape),
        ],
        out_specs=(
            full((lay.spread, lay.tokens, width)),
            full((3 * feats, width)),
            pl.BlockSpec((1, 1, span), lambda h: (h, 0, 0)),
        ),
        out_shape=(
            jax.ShapeDtypeStruct((lay.spread, lay.tokens, width), BF16),
            jax.ShapeDtypeStruct((3 * feats, width), F32),
            jax.ShapeDtypeStruct((heads, 1, span), F32),
        ),
        scratch_shapes=[
            VMEM((lay.tiles, BK, BK), BF16),
            VMEM((HD, lay.total), BF16),
            VMEM((lay.total, HD), BF16),
            VMEM((3 * feats, lay.total), BF16),
        ],
        compiler_params=pltpu.CompilerParams(vmem_limit_bytes=58 * MIB),
        name="attention_backward",
    )(dattn_t, e, qkvn, qkvt, ot, rl, h1, weights_t)


def finish_kernel(dh1_ref, x_ref, gain_ref, dmid_ref, dx_ref, ggain_ref):
    x = x_ref[...].astype(F32)
    dh1 = dh1_ref[...].astype(F32)
    r = lax.rsqrt(jnp.mean(x * x, axis=1, keepdims=True) + EPSILON)
    w = dh1 * gain_ref[...]
    mean = jnp.mean(w * x, axis=1, keepdims=True)
    dx_ref[...] = dmid_ref[...] + r * w - (r * r * r) * x * mean
    ggain_ref[...] = jnp.sum(dh1 * x * r, axis=0, keepdims=True)


def finish(dh1, x_local, gain, dmid):
    return pl.pallas_call(
        finish_kernel,
        out_shape=(
            jax.ShapeDtypeStruct(dmid.shape, F32),
            jax.ShapeDtypeStruct((1, dmid.shape[1]), F32),
        ),
        compiler_params=pltpu.CompilerParams(vmem_limit_bytes=32 * MIB),
        name="finish",
    )(dh1, x_local, gain, dmid)


def result_kernel(mid_ref, cols_ref, gates_ref, made_ref, out_ref):
    tokens = mid_ref.shape[0]
    slots = made_ref.shape[0]
    lane = lax.broadcasted_iota(jnp.int32, (tokens, slots), 1)
    out = mid_ref[...]
    for i in range(2):
        pick = jnp.where(cols_ref[:, i : i + 1] == lane, 1.0, 0.0).astype(BF16)
        out = out + gates_ref[:, i : i + 1] * dot(pick, made_ref[...])
    out_ref[...] = out.astype(BF16)


def result(mid, cols, gates, made):
    return pl.pallas_call(
        result_kernel,
        out_shape=jax.ShapeDtypeStruct(mid.shape, BF16),
        compiler_params=pltpu.CompilerParams(vmem_limit_bytes=32 * MIB),
        name="result",
    )(mid, cols, gates, made)


def body(
    prompt_in,
    cont_in,
    prompt_route,
    cont_route,
    order,
    buckets,
    attn_gain,
    w_query,
    w_key,
    w_value,
    w_attn_out,
    rel_bias,
    ffn_gain,
    router,
    w_in,
    w_out,
    prompt_cot,
    cont_cot,
):
    prompt_rows = prompt_in.shape[1]
    cont_count = cont_in.shape[1]
    cont_rows = cont_in.shape[2]
    width = prompt_in.shape[2]
    spread = lax.axis_size("context")
    expert_devices = lax.axis_size("expert")
    lay = Layout(spread, prompt_rows, cont_count, cont_rows)
    tokens = lay.tokens
    head_count = rel_bias.shape[1]
    heads = head_count // spread
    feats = heads * HD
    experts = w_in.shape[0] * expert_devices
    capacity = 9 * tokens * 2 // (8 * experts)
    slots = experts * capacity
    buckets_count = rel_bias.shape[0]
    context = lax.axis_index("context")

    def local_rows(prompt_part, cont_part):
        return jnp.concatenate(
            [prompt_part.reshape(prompt_rows, -1), cont_part.reshape(cont_count * cont_rows, -1)],
            axis=0,
        )

    def own_columns(matrix):
        return lax.dynamic_slice_in_dim(matrix, context * feats, feats, 1)

    def exchange(array, axis):
        return lax.all_to_all(array, axis, split_axis=0, concat_axis=0, tiled=True)

    x_local = local_rows(prompt_in, cont_in)
    x_all = lax.all_gather(x_local, "context", axis=0, tiled=False)
    routes = local_rows(prompt_route, cont_route)
    upstream = local_rows(prompt_cot, cont_cot)
    gain_one = attn_gain.reshape(1, width)
    gain_two = ffn_gain.reshape(1, width)
    slot_rows, slot_cols, dz_slots = plan(routes, order.reshape(tokens), upstream, experts, capacity)
    dz_slots = exchange(dz_slots.reshape(expert_devices, slots // expert_devices, -1), "expert")
    dz_slots = dz_slots.reshape(slots, -1)

    bucket_hot = (buckets[:, None] == jnp.arange(buckets_count, dtype=jnp.int32)[None, :]).astype(F32)
    own_bias = lax.dynamic_slice_in_dim(rel_bias, context * heads, heads, 1)
    table = jnp.dot(bucket_hot, own_bias, precision=PRECISE).T
    table = jnp.pad(table, ((0, 0), (BK, 0))).reshape(heads, 1, -1)
    weights = jnp.concatenate([own_columns(w) for w in (w_query, w_key, w_value)], axis=1)
    weights_t = weights.T
    h1, qkvn, qkvt, e, ot, rl, at = attention_forward(lay, heads, x_all, gain_one, weights, table)
    attended_t = exchange(at, "context").reshape(width, tokens)
    mid, h2, gates, sent = middle(
        attended_t, x_local, w_attn_out, gain_two, router, routes, slot_rows, experts, capacity
    )
    arrived = exchange(sent.reshape(expert_devices, slots // expert_devices, width), "expert")
    arrived = arrived.reshape(slots, width)
    act, dpre, dsent, dmade, share = expert_grad(arrived, dz_slots, router, w_in, w_out)
    dsent = exchange(dsent.reshape(expert_devices, slots // expert_devices, width), "expert")
    share = exchange(share[:, 0].reshape(expert_devices, slots // expert_devices), "expert")
    made, g_in, g_out = expert_weights(arrived, dmade, act, dpre, w_out)
    dmid, dattn_t, g_wo, g_gain_two, g_router = turn(
        dsent.reshape(slots, width),
        share.reshape(1, slots),
        slot_cols,
        gates,
        routes,
        mid,
        upstream,
        h2,
        gain_two,
        router,
        w_attn_out,
        attended_t,
    )
    dattn_t = exchange(dattn_t.reshape(spread, feats, tokens), "context")
    made = exchange(made.reshape(expert_devices, slots // expert_devices, width), "expert")
    g_in_sum, g_out_sum = (
        lax.psum_scatter(g, ("dp", "context"), scatter_dimension=1, tiled=True).astype(F32)
        for g in (g_in, g_out)
    )
    dh1, g_qkv, g_table = attention_backward(
        lay, heads, dattn_t, e, qkvn, qkvt, ot, rl, h1, weights_t
    )
    dh1 = lax.psum_scatter(dh1, "context", scatter_dimension=0, tiled=False)
    dx, g_gain_one = finish(dh1, x_local, gain_one, dmid)
    out = result(mid, slot_cols, gates, made.reshape(slots, width))

    g_bias = jnp.dot(g_table[:, 0, BK:], bucket_hot, precision=PRECISE)
    g_bias = lax.dynamic_update_slice_in_dim(
        jnp.zeros((head_count, width), F32), jnp.pad(g_bias, ((0, 0), (0, width - buckets_count))), context * heads, 0
    )
    small = jnp.concatenate([g_gain_one, g_gain_two, g_router, g_bias], axis=0)
    g_wo, small = lax.psum((g_wo, small), ("dp", "context", "expert"))
    g_qkv = lax.psum(g_qkv, ("dp", "expert"))
    g_qkv = lax.all_gather(g_qkv, "context", axis=0, tiled=False)
    g_qkv = g_qkv.reshape(spread, 3, feats, width)
    g_query, g_key, g_value = (g_qkv[:, i].reshape(width, width).T for i in range(3))
    g_bias = small[2 + experts :, :buckets_count].T
    g_router = small[2 : 2 + experts].T
    return (
        out[:prompt_rows].reshape(1, prompt_rows, width),
        out[prompt_rows:].reshape(1, cont_count, cont_rows, width),
        dx[:prompt_rows].reshape(1, prompt_rows, width),
        dx[prompt_rows:].reshape(1, cont_count, cont_rows, width),
        small[0],
        g_query,
        g_key,
        g_value,
        g_wo,
        g_bias,
        small[1],
        g_router,
        g_in_sum,
        g_out_sum,
    )


def solution(mesh):
    split = P(("dp", "expert"), "context", None)
    split_cont = P(("dp", "expert"), None, "context", None)
    whole = P()
    expert = P("expert", None, None)
    grad = P("expert", ("dp", "context"), None)
    return jax.shard_map(
        body,
        mesh=mesh,
        in_specs=(split, split_cont, split, split_cont, split)
        + (whole,) * 9
        + (expert, expert, split, split_cont),
        out_specs=(split, split_cont, split, split_cont) + (whole,) * 8 + (grad, grad),
        check_vma=False,
    )
```

time: 2020 us -> 785 us (0.39)
  local copies, waits for them, and re-layouts: 1040 us -> 47.9 us
  matrix products: 255 us -> 1.76 us
  other arithmetic: 248 us -> 8.2 us
  Pallas kernels: 0 us -> 126 us
  blocking collectives: 42.3 us -> 162 us
  waiting for transfers between devices: 343 us -> 406 us
  loops' own time: 31.7 us -> 0 us
    scatter x38 -> x0, local copies, waits for them, and re-layouts: 285 us -> none  [the longest x36 276 us: build_bias(): result = result.at[:, q_off:q_off + q_len, k_off:k_off + k_len].set(tile)]
    dot_general x67 -> x2, matrix products: 255 us -> 1.76 us  [the longest x1 1.29 us: body(): table = jnp.dot(bucket_hot, own_bias, precision=PRECISE).T]
    reshape x114 -> x4, local copies, waits for them, and re-layouts: 223 us -> 1.98 us  [the longest x1 0.77 us: body(): share.reshape(1, slots)]
    pallas_call x0 -> x9, Pallas kernels: none -> 126 us  [the longest x1 29.9 us: attention_backward(): pl.pallas_call(functools.partial(attention_back_kernel, lay, heads), grid...]
    all_to_all x0 -> x4, blocking collectives: none -> 122 us  [exchange(): return lax.all_to_all(array, axis, split_axis=0, concat_axis=0, tiled=True)]
    concatenate x196 -> x1, local copies, waits for them, and re-layouts: 94.4 us -> 1.31 us  [body(): jnp.concatenate([own_columns(w) for w in (w_query, w_key, w_value)], axis=1)]
    dynamic_update_slice x120 -> x1, local copies, waits for them, and re-layouts: 88.5 us -> 0.25 us  [body(): lax.dynamic_update_slice_in_dim(jnp.zeros((head_count, width), F32), jnp....]
    while x330 -> x0, local copies, waits for them, and re-layouts: 83.3 us -> none
  transfers between devices with their start and end apart: 11 -> 10, of which waited for: 9 -> 10; matrix products, arithmetic and copies ran while one was open for 38% -> 4% of each run, Pallas kernels for 0% -> 4%
where the time goes in v1:
time: 785 us; the launch traced here: 780 us
  waiting for transfers between devices  406 us (52%)
  blocking collectives  162 us (21%)
  Pallas kernels  126 us (16%)
  local copies, waits for them, and re-layouts  47.9 us (6%)
  between operations  14.8 us (2%)
  starting transfers between devices  13.3 us (2%)
  other arithmetic  8.2 us (1%)
    psum x1, waiting for transfers between devices, body(): g_wo, small = lax.psum((g_wo, small), ('dp', 'context', 'expert'))  127 us
    all_to_all x4, blocking collectives, exchange(): return lax.all_to_all(array, axis, split_axis=0, concat_axis=0, tiled=True)  122 us
    all_to_all x3, waiting for transfers between devices, exchange(): return lax.all_to_all(array, axis, split_axis=0, concat_axis=0, tiled=True)  80.5 us
    psum x1, waiting for transfers between devices, body(): g_qkv = lax.psum(g_qkv, ('dp', 'expert'))  66.1 us
    reduce_scatter x2, waiting for transfers between devices, body(): lax.psum_scatter(g, ('dp', 'context'), scatter_dimension=1, tiled=True)  63.6 us
    psum x1, blocking collectives, body(): g_wo, small = lax.psum((g_wo, small), ('dp', 'context', 'expert'))  40.4 us
    reduce_scatter x1, waiting for transfers between devices, body(): dh1 = lax.psum_scatter(dh1, 'context', scatter_dimension=0, tiled=False)  38.3 us
    pallas_call x1, Pallas kernels, attention_backward(): pl.pallas_call(functools.partial(attention_back_kernel, lay, heads), grid...  29.9 us
  transfers between devices with their start and end apart: 10, of which 10 were waited for; matrix products, arithmetic and copies ran while one was open for 4% of the time, Pallas kernels for 4%

profile of v1, /device:TPU:0, one launch (start us, length us, event | category | flops | bytes accessed | tf_op | source)
XLA Modules:
  0.0 780.4 jit_solution(12860460142545783542)
XLA Ops:
  16.5 24.9 %all-gather.6.cloned.1.call-done = bf16[2048,768]{1,0:T(8,128)(2,1)} async-done(((bf16[512,768]{1,0:T(8,128)(2,1)}), bf16[2048,768]{1,0:T(8,128)(2,1)}) %all-gather.6.cloned.1.call-update) | async-done | bytes 3145744 | tf_op jit(solution)/shard_map/all_gather | solution.py:687
  41.4 25.8 %attention_forward.1 = (bf16[2048,768]{1,0:T(8,128)(2,1)}, bf16[9,2048,64]{2,1,0:T(8,128)(2,1)}, bf16[576,2048]{1,0:T(8,128)(2,1)}, bf16[3,32,256,256]{3,2,1,0:T...) custom-call(bf16[4,512,768]{2,1,0:T(8,128)(2,1)} %bitcast.63, ...), custom_call_target="tpu_custom_call" | custom-call | tf_op jit(solution)/shard_map/attention_forward/pallas_call | solution.py:227
  67.3 3.9 all-to-all-start
  71.7 2.9 slot_plan.1
  77.2 5.6 all-to-all-done
  82.8 4.7 all-to-all-start.2
  91.0 3.1 middle.1
  98.1 37.0 %all-to-all-done.2 = bf16[4,288,896]{2,1,0:T(8,128)(2,1)} async-done(((bf16[4,288,896]{2,1,0:T(8,128)(2,1)}), bf16[4,288,896]{2,1,0:T(8,128)(2,1)}, u32[]{:S(2)}, u32[]{:S(2)}) %all-to-all-start.2) | async-done | bytes 2064416 | tf_op jit(solution)/shard_map/all_to_all | solution.py:684
  135.1 45.1 %all_to_all.40 = bf16[4,288,768]{2,1,0:T(8,128)(2,1)} all-to-all(bf16[4,288,768]{2,1,0:T(8,128)(2,1)} %bitcast.52), channel_id=1, replica_groups=mesh['dp'=2,'context'=4,'expert'=4] {'expert'}, dimensions={0} | all-to-all | bytes 3538944 | tf_op jit(solution)/shard_map/all_to_all | solution.py:684
  180.2 28.6 %expert_grad.1 = (bf16[1152,3072]{1,0:T(8,128)(2,1)}, bf16[1152,3072]{1,0:T(8,128)(2,1)}, bf16[1152,768]{1,0:T(8,128)(2,1)}, bf16[1152,768]{1,0:T(8,128)(2,1)}, f32[1152,128]{1,0:T(8,128)}) custom-call(bf16[1152,768]{1,0:T(8,128)(2,1)} %bitcast.57, bf16[1152,896]{1,0:T(8,128)(2,1)} %bitcast.14.dzp_ref, bf16[768,4]{1,0:T(8,128)(2,1)} %copy.85.router_ref, ...), custom_call_target="tpu_custom_call" | custom-call | tf_op jit(solution)/shard_map/expert_grad/pallas_call | solution.py:364
  210.8 8.8 %all_to_all.41 = f32[4,1,288]{2,1,0:T(1,128)S(1)} all-to-all(f32[4,1,288]{2,1,0:T(1,128)} %all_to_all.32), channel_id=1, replica_groups=mesh['dp'=2,'context'=4,'expert'=4] {'expert'}, dimensions={0} | all-to-all | bytes 9216 | tf_op jit(solution)/shard_map/all_to_all | solution.py:684
  219.6 4.4 all-to-all-start.4
  225.4 37.9 %all-to-all-done.4 = bf16[4,288,768]{2,1,0:T(8,128)(2,1)} async-done(((bf16[4,288,768]{2,1,0:T(8,128)(2,1)}), bf16[4,288,768]{2,1,0:T(8,128)(2,1)}, u32[]{:S(2)}, u32[]{:S(2)}) %all-to-all-start.4) | async-done | bytes 1769504 | tf_op jit(solution)/shard_map/all_to_all | solution.py:684
  268.2 8.1 %turn.1 = (f32[512,768]{1,0:T(8,128)}, bf16[768,512]{1,0:T(8,128)(2,1)S(1)}, f32[768,768]{1,0:T(8,128)}, f32[1,768]{1,0:T(1,128)S(1)}, f32[4,768]{1,0:T(4,128)S(1)}) custom-call(bf16[1152,768]{1,0:T(8,128)(2,1)} %bitcast.20.dsent_ref, f32[1,1152]{1,0:T(1,128)S(1)} %reshape.128.share_ref, s32[512,128]{1,0:T(8,128)S(1)} %copy-done.16, ...), custom_call_target="tpu_custom_call" | custom-call | tf_op jit(solution)/shard_map/turn/pallas_call | solution.py:478
  276.3 23.1 %all_to_all.42.dot_ref = bf16[4,192,512]{2,1,0:T(8,128)(2,1)} all-to-all(bf16[4,192,512]{2,1,0:T(8,128)(2,1)S(1)} %bitcast.53), channel_id=1, replica_groups=mesh['dp'=2,'context'=4,'expert'=4] {'context'}, dimensions={0} | all-to-all | bytes 1572864 | tf_op jit(solution)/shard_map/all_to_all | solution.py:684
  299.4 29.9 %attention_backward.1 = (bf16[4,512,768]{2,1,0:T(8,128)(2,1)}, f32[576,768]{1,0:T(8,128)}, f32[3,1,1792]{2,1,0:T(1,128)}) custom-call(bf16[4,192,512]{2,1,0:T(8,128)(2,1)} %all_to_all.42.dot_ref, bf16[3,32,256,256]{3,2,1,0:T(8,128)(2,1)} %get-tuple-element.61.e_ref, bf16[9,2048,64]{2,1,0:T(8,128)(2,1)} %get-tuple-element.62.qkvn_ref, ...), custom_call_target="tpu_custom_call" | custom-call | tf_op jit(solution)/shard_map/attention_backward/pallas_call | solution.py:561
  329.4 24.4 %expert_weights.1 = (bf16[1152,768]{1,0:T(8,128)(2,1)}, bf16[1,768,3072]{2,1,0:T(8,128)(2,1)}, bf16[1,3072,768]{2,1,0:T(8,128)(2,1)}) custom-call(bf16[1152,768]{1,0:T(8,128)(2,1)} %bitcast.58, bf16[1152,768]{1,0:T(8,128)(2,1)} %get-tuple-element.53.dmade_ref, bf16[1152,3072]{1,0:T(8,128)(2,1)} %get-tuple-element.54.act_ref, ...), custom_call_target="tpu_custom_call" | custom-call | tf_op jit(solution)/shard_map/expert_weights/pallas_call | solution.py:417
  355.1 66.1 %all-reduce.5.cloned.1.call-done = f32[1,576,768]{2,1,0:T(8,128)} async-done(((f32[1,576,768]{2,1,0:T(8,128)}), f32[1,576,768]{2,1,0:T(8,128)}) %all-reduce.5.cloned.1.call-update) | async-done | bytes 1769488 | tf_op jit(solution)/shard_map/psum | solution.py:746
  421.3 44.6 %all_to_all.43 = bf16[4,288,768]{2,1,0:T(8,128)(2,1)S(1)} all-to-all(bf16[4,288,768]{2,1,0:T(8,128)(2,1)S(1)} %bitcast.65), channel_id=1, replica_groups=mesh['dp'=2,'context'=4,'expert'=4] {'expert'}, dimensions={0} | all-to-all | bytes 3538944 | tf_op jit(solution)/shard_map/all_to_all | solution.py:684
  465.8 2.2 result.1
  469.9 8.6 %reduce-scatter.6.cloned.1.call-done = bf16[1,96,3072]{2,1,0:T(8,128)(2,1)} async-done(((bf16[1,768,3072]{2,1,0:T(8,128)(2,1)}), bf16[1,96,3072]{2,1,0:T(8,128)(2,1)}) %reduce-scatter.6.cloned.1.call-update) | async-done | bytes 589840 | tf_op jit(solution)/shard_map/reduce_scatter | solution.py:730
  478.5 2.2 convert_element_type.11
  480.7 55.1 %reduce-scatter.8.cloned.1.call-done = bf16[1,384,768]{2,1,0:T(8,128)(2,1)} async-done(((bf16[1,3072,768]{2,1,0:T(8,128)(2,1)}), bf16[1,384,768]{2,1,0:T(8,128)(2,1)}) %reduce-scatter.8.cloned.1.call-update) | async-done | bytes 589840 | tf_op jit(solution)/shard_map/reduce_scatter | solution.py:730
  537.9 38.3 %reduce-scatter.4.cloned.1.call-done = bf16[1,512,768]{2,1,0:T(8,128)(2,1)} async-done(((bf16[4,512,768]{2,1,0:T(8,128)(2,1)}), bf16[1,512,768]{2,1,0:T(8,128)(2,1)}) %reduce-scatter.4.cloned.1.call-update) | async-done | bytes 786448 | tf_op jit(solution)/shard_map/reduce_scatter | solution.py:736
  579.4 40.4 %psum.21 = f32[18,768]{1,0:T(8,128)S(1)} all-reduce(f32[18,768]{1,0:T(8,128)S(1)} %pad_maximum_fusion.3), channel_id=1, replica_groups=mesh['dp'=2,'context'=4,'expert'=4] {'dp','context','expert'}, use_global_device_ids=true, to_apply=%region_1.2 | all-reduce | flops 13824 | bytes 110592 | tf_op jit(solution)/shard_map/psum | solution.py:745
  621.7 2.6 fusion.11
  624.3 5.1 all-gather.4.cloned.1.call-done
  629.4 5.9 fusion.10
  635.3 3.0 copy.91
  638.3 3.0 copy.92
  643.3 126.7 %all-reduce.7.cloned.1.call-done = f32[768,768]{1,0:T(8,128)} async-done(((f32[768,768]{1,0:T(8,128)}), f32[768,768]{1,0:T(8,128)}) %all-reduce.7.cloned.1.call-update) | async-done | bytes 2359312 | tf_op jit(solution)/shard_map/psum | solution.py:745
  770.0 3.3 copy.105
  (131 shorter events, 40.1 us)
Async XLA Ops:
  7.2 4.1 copy-start
  7.2 34.2 %all-gather.6.cloned.1.call-start = ((), (), s32[]{:S(2)}) async-start(), calls=%async_computation.16 | async-start | bytes 3932160 | tf_op jit(solution)/shard_map/all_gather | solution.py:687
  11.7 2.4 copy-start.39
  11.7 4.3 copy-start.35
  41.4 29.8 %copy-start.37 = (s32[1,2,128,2]{2,3,1,0:T(2,128)S(1)}, s32[1,2,128,2]{2,3,1,0:T(2,128)}, u32[]{:S(2)}) copy-start(s32[1,2,128,2]{2,3,1,0:T(2,128)} %param.21) | copy-start | bytes 6148
  41.4 29.8 %copy-start.38 = (s32[1,256,2]{1,2,0:T(2,128)S(1)}, s32[1,256,2]{1,2,0:T(2,128)}, u32[]{:S(2)}) copy-start(s32[1,256,2]{1,2,0:T(2,128)} %param.20) | copy-start | bytes 6148
  67.3 4.1 copy-start.29
  67.3 4.3 copy-start.31
  67.3 4.3 copy-start.32
  67.3 15.5 %all-to-all-start = ((bf16[4,192,512]{2,1,0:T(8,128)(2,1)}), bf16[4,192,512]{2,1,0:T(8,128)(2,1)S(1)}, u32[]{:S(2)}, u32[]{:S(2)}) async-start(bf16[4,192,512]{2,1,0:T(8,128)(2,1)} %get-tuple-element.46), calls=%async_computation | async-start | bytes 1572864 | tf_op jit(solution)/shard_map/all_to_all | solution.py:684
  71.4 11.4 %copy-start.6 = (s32[512,2]{1,0:T(8,128)}, s32[512,2]{1,0:T(8,128)S(1)}, u32[]{:S(2)}) copy-start(s32[512,2]{1,0:T(8,128)S(1)} %copy.86.route_ref) | copy-start | bytes 12292
  82.8 4.8 copy-start.34
  82.8 5.6 copy-start.36
  82.8 5.6 copy-start.2
  82.8 5.6 copy-start.5
  82.8 52.2 %all-to-all-start.2 = ((bf16[4,288,896]{2,1,0:T(8,128)(2,1)}), bf16[4,288,896]{2,1,0:T(8,128)(2,1)}, u32[]{:S(2)}, u32[]{:S(2)}) async-start(bf16[4,288,896]{2,1,0:T(8,128)(2,1)} %bitcast.51), calls=%async_computation.2 | async-start | bytes 4128768 | tf_op jit(solution)/shard_map/all_to_all | solution.py:684
  219.6 43.7 %all-to-all-start.4 = ((bf16[4,288,768]{2,1,0:T(8,128)(2,1)}), bf16[4,288,768]{2,1,0:T(8,128)(2,1)}, u32[]{:S(2)}, u32[]{:S(2)}) async-start(bf16[4,288,768]{2,1,0:T(8,128)(2,1)} %bitcast.66), calls=%async_computation.4 | async-start | bytes 3538944 | tf_op jit(solution)/shard_map/all_to_all | solution.py:684
  223.9 197.2 %all-reduce.5.cloned.1.call-start = ((), (), s32[]{:S(2)}) async-start(), calls=%async_computation.11 | async-start | bytes 3538944 | tf_op jit(solution)/shard_map/psum | solution.py:746
  276.3 23.1 %copy-start.27 = (f32[4,768]{1,0:T(4,128)}, f32[4,768]{1,0:T(4,128)S(1)}, u32[]{:S(2)}) copy-start(f32[4,768]{1,0:T(4,128)S(1)} %get-tuple-element.72) | copy-start | bytes 36868
  329.3 149.2 %reduce-scatter.6.cloned.1.call-start = ((), (), s32[]{:S(2)}) async-start(), calls=%async_computation.14 | async-start | bytes 5308416 | tf_op jit(solution)/shard_map/reduce_scatter | solution.py:730
  353.9 181.9 %reduce-scatter.8.cloned.1.call-start = ((), (), s32[]{:S(2)}) async-start(), calls=%async_computation.15 | async-start | bytes 5308416 | tf_op jit(solution)/shard_map/reduce_scatter | solution.py:730
  354.4 221.8 %reduce-scatter.4.cloned.1.call-start = ((), (), s32[]{:S(2)}) async-start(), calls=%async_computation.10 | async-start | bytes 3932160 | tf_op jit(solution)/shard_map/reduce_scatter | solution.py:736
  354.5 66.8 %copy-start.30 = (bf16[1152,768]{1,0:T(8,128)(2,1)S(1)}, bf16[1152,768]{1,0:T(8,128)(2,1)}, u32[]{:S(2)}) copy-start(bf16[1152,768]{1,0:T(8,128)(2,1)} %get-tuple-element.56) | copy-start | bytes 5308420
  355.0 274.4 %all-gather.4.cloned.1.call-start = ((), (), s32[]{:S(2)}) async-start(), calls=%async_computation.12 | async-start | bytes 8847360 | tf_op jit(solution)/shard_map/all_gather | solution.py:747
  421.2 348.8 %all-reduce.7.cloned.1.call-start = ((), (), s32[]{:S(2)}) async-start(), calls=%async_computation.13 | async-start | bytes 4718592 | tf_op jit(solution)/shard_map/psum | solution.py:745
  421.2 44.6 %copy-start.4 = (f32[512,768]{1,0:T(8,128)S(1)}, f32[512,768]{1,0:T(8,128)}, u32[]{:S(2)}) copy-start(f32[512,768]{1,0:T(8,128)} %copy-done.3) | copy-start | bytes 4718596
  421.2 44.6 %copy-start.17 = (s32[512,128]{1,0:T(8,128)S(1)}, s32[512,128]{1,0:T(8,128)}, u32[]{:S(2)}) copy-start(s32[512,128]{1,0:T(8,128)} %copy-done.15) | copy-start | bytes 786436
  421.3 44.6 %copy-start.20 = (f32[512,128]{1,0:T(8,128)S(1)}, f32[512,128]{1,0:T(8,128)}, u32[]{:S(2)}) copy-start(f32[512,128]{1,0:T(8,128)} %copy-done.18) | copy-start | bytes 786436
  469.9 106.3 %copy-start.13 = (f32[512,768]{1,0:T(8,128)S(1)}, f32[512,768]{1,0:T(8,128)}, u32[]{:S(2)}) copy-start(f32[512,768]{1,0:T(8,128)} %get-tuple-element.68.dmid_ref) | copy-start | bytes 4718596
  469.9 106.3 %copy-start.24 = (f32[1,768]{1,0:T(1,128)S(1)}, f32[1,768]{1,0:T(1,128)}, u32[]{:S(2)}) copy-start(f32[1,768]{1,0:T(1,128)} %reshape.110.gain_ref) | copy-start | bytes 9220
  535.7 43.6 %copy-start.28 = (f32[4,768]{1,0:T(4,128)S(1)}, f32[4,768]{1,0:T(4,128)}, u32[]{:S(2)}) copy-start(f32[4,768]{1,0:T(4,128)} %copy-done.27) | copy-start | bytes 36868
  770.0 3.3 copy-start.1
  (19 other events, 18.3 us)
Sparse Core Ops, SparseCore 0:
  10.2 31.2 all-gather.5
  329.5 91.6 all-reduce.4
  425.0 53.4 reduce-scatter.5
  481.8 53.8 reduce-scatter.7
  538.3 37.9 reduce-scatter.3
  577.6 51.7 all-gather.3
  635.0 134.9 all-reduce.6

commit v2 on v1

--- a/solution.py
+++ b/solution.py
@@ -15,6 +15,7 @@
 BF16 = jnp.bfloat16
 PRECISE = lax.Precision.HIGHEST
 VMEM = pltpu.VMEM
+MESH = pl.DeviceIdType.MESH
 MIB = 1 << 20
 
 
@@ -79,65 +80,53 @@
         return self.place[q] - self.place[k]
 
 
-def plan_kernel(
-    experts, capacity, route_ref, route_t_ref, order_row_ref, order_col_ref, dz_ref, rows_ref, cols_ref, dzp_ref
-):
-    tokens = dz_ref.shape[0]
-    slots = experts * capacity
+def flip(index, mask):
+    bit = 1
+    while bit <= mask:
+        if mask & bit:
+            index = index + bit * (1 - 2 * ((index // bit) % 2))
+        bit *= 2
+    return index
+
+
+def remote(src, dst, send, recv, **where):
+    return pltpu.make_async_remote_copy(
+        src_ref=src,
+        dst_ref=dst,
+        send_sem=send,
+        recv_sem=recv,
+        device_id=where,
+        device_id_type=MESH,
+    )
+
+
+def greet(partners):
+    barrier = pltpu.get_barrier_semaphore()
+    for where in partners:
+        pl.semaphore_signal(barrier, inc=1, device_id=where, device_id_type=MESH)
+    pl.semaphore_wait(barrier, len(partners))
+
+
+def make_plan(capacity, routes, order_row):
+    tokens = routes.shape[0]
     side = (tokens, tokens)
-    lane = lax.broadcasted_iota(jnp.int32, side, 1)
+    lane = lax.broadcasted_iota(jnp.int32, side, 1).astype(F32)
     sub = lax.broadcasted_iota(jnp.int32, side, 0)
-    rank_col = jnp.sum(
-        jnp.where(order_row_ref[...] == sub, lane, 0).astype(F32), axis=1, keepdims=True
-    )
-    rank_row = jnp.sum(
-        jnp.where(order_col_ref[...] == lane, sub, 0).astype(F32), axis=0, keepdims=True
-    )
+    rank_col = jnp.sum(jnp.where(order_row == sub, lane, 0.0), axis=1, keepdims=True)
+    rank_row = jnp.broadcast_to(rank_col, (tokens, 128)).T[0:1]
     before = jnp.where(rank_row < rank_col, 1.0, 0.0).astype(BF16)
-    before_t = jnp.where(rank_col < rank_row, 1.0, 0.0).astype(BF16)
-    expert_lane = lax.broadcasted_iota(jnp.int32, (tokens, 128), 1)
-    hots = [jnp.where(route_ref[:, i : i + 1] == expert_lane, 1.0, 0.0) for i in range(2)]
+    expert_lane = lax.broadcasted_iota(jnp.int32, (tokens, 128), 1).astype(F32)
+    hots = [jnp.where(routes[:, i : i + 1] == expert_lane, 1.0, 0.0) for i in range(2)]
     counts = [dot(before, hot.astype(BF16)) for hot in hots]
     counts[1] = counts[1] + jnp.sum(hots[0], axis=0, keepdims=True)
-    expert_sub = lax.broadcasted_iota(jnp.int32, (16, tokens), 0)
-    hots_t = [jnp.where(route_t_ref[i : i + 1, :] == expert_sub, 1.0, 0.0) for i in range(2)]
-    counts_t = [dot(hot.astype(BF16), before_t) for hot in hots_t]
-    counts_t[1] = counts_t[1] + jnp.sum(hots_t[0], axis=1, keepdims=True)
-    slot_rows = []
-    cols = jnp.full((tokens, 128), -1, jnp.int32)
+    cols = jnp.zeros((tokens, 128), F32)
     for i in range(2):
-        pos = jnp.sum(hots[i] * counts[i], axis=1, keepdims=True).astype(jnp.int32)
-        slot = jnp.where(pos < capacity, route_ref[:, i : i + 1] * capacity + pos, -1)
+        pos = jnp.sum(hots[i] * counts[i], axis=1, keepdims=True)
+        route = routes[:, i : i + 1]
+        slot = jnp.where(pos < capacity, route * capacity + pos, -1.0)
         cols = jnp.where(expert_lane == i, slot, cols)
-        pos = jnp.sum(hots_t[i] * counts_t[i], axis=0, keepdims=True).astype(jnp.int32)
-        slot_rows.append(jnp.where(pos < capacity, route_t_ref[i : i + 1, :] * capacity + pos, -1))
-    cols_ref[...] = cols
-    sub8 = lax.broadcasted_iota(jnp.int32, (8, tokens), 0)
-    rows_ref[...] = jnp.where(sub8 == 0, slot_rows[0], jnp.where(sub8 == 1, slot_rows[1], -1))
-    dz = dz_ref[...]
-    for start in range(0, slots, 128):
-        number = lax.broadcasted_iota(jnp.int32, (128, tokens), 0) + start
-        first = jnp.where(slot_rows[0] == number, 1.0, 0.0)
-        second = jnp.where(slot_rows[1] == number, 1.0, 0.0)
-        dzp_ref[start : start + 128, : dz.shape[1]] = dot((first + second).astype(BF16), dz).astype(BF16)
-        other = dot(first.astype(BF16), hots[1].astype(BF16)) + dot(
-            second.astype(BF16), hots[0].astype(BF16)
-        )
-        dzp_ref[start : start + 128, dz.shape[1] :] = other.astype(BF16)
-
-
-def plan(routes, ranking, upstream, experts, capacity):
-    tokens, width = upstream.shape
-    return pl.pallas_call(
-        functools.partial(plan_kernel, experts, capacity),
-        out_shape=(
-            jax.ShapeDtypeStruct((8, tokens), jnp.int32),
-            jax.ShapeDtypeStruct((tokens, 128), jnp.int32),
-            jax.ShapeDtypeStruct((experts * capacity, width + 128), BF16),
-        ),
-        compiler_params=pltpu.CompilerParams(vmem_limit_bytes=32 * MIB),
-        name="slot_plan",
-    )(routes, routes.T, ranking.reshape(1, tokens), ranking.reshape(tokens, 1), upstream)
+        cols = jnp.where(expert_lane == 2 + i, route, cols)
+    return cols, cols.T[0:8], hots
 
 
 def toeplitz_tile(table_row, d):
@@ -172,31 +161,172 @@
     return jnp.sum(tile, axis=0, keepdims=True)
 
 
-def attention_kernel(
-    lay, heads, x_ref, gain_ref, w_ref, tab_ref, h1_ref, qkvn_ref, qkvt_ref, e_ref, ot_ref, rl_ref, at_ref, s_scr, bias_scr
+def front_kernel(
+    lay,
+    heads,
+    peers,
+    capacity,
+    xp_ref,
+    xc_ref,
+    rp_ref,
+    rc_ref,
+    order_ref,
+    buckets_ref,
+    gain_ref,
+    wq_ref,
+    wk_ref,
+    wv_ref,
+    bias_ref,
+    zp_ref,
+    zc_ref,
+    h1_ref,
+    qkvn_ref,
+    qkvt_ref,
+    e_ref,
+    ot_ref,
+    rl_ref,
+    w_ref,
+    cols_ref,
+    rows_ref,
+    at_ref,
+    dz_ref,
+    x_all,
+    at_scr,
+    dz_scr,
+    s_scr,
+    bias_scr,
+    x_send,
+    x_recv,
+    a_send,
+    a_recv,
+    z_send,
+    z_recv,
+    own_sem,
 ):
     h = pl.program_id(0)
+    me = lax.axis_index("context")
+    expert = lax.axis_index("expert")
+    feats = heads * HD
+    half = lay.prompt_rows
+    near, across, far = flip(me, 1), flip(me, 2), flip(me, 3)
+    width = gain_ref.shape[1]
+
+    def x_copy(slot, part, index, target):
+        view = x_all.at[slot, pl.ds(part * half, half)]
+        return remote(view, view, x_send.at[index], x_recv.at[index], context=target)
+
+    def z_copy(k):
+        return remote(
+            dz_scr.at[k], dz_ref.at[k], z_send.at[k], z_recv.at[k], expert=flip(expert, k)
+        )
+
+    def a_copy(k, head):
+        target = flip(me, k)
+        src = at_scr.at[target, pl.ds(head * HD, HD)]
+        dst = at_ref.at[me, pl.ds(head * HD, HD)]
+        return remote(src, dst, a_send.at[head, k], a_recv.at[head, k], context=target)
+
+    def a_own(head):
+        return pltpu.make_async_copy(
+            at_scr.at[me, pl.ds(head * HD, HD)],
+            at_ref.at[me, pl.ds(head * HD, HD)],
+            a_send.at[head, 0],
+        )
+
+    z_own = pltpu.make_async_copy(dz_scr.at[0], dz_ref.at[0], own_sem)
+
+    def project(slot):
+        x = x_all[slot].astype(F32)
+        r = lax.rsqrt(jnp.mean(x * x, axis=1, keepdims=True) + EPSILON)
+        normed = (x * r * gain_ref[...]).astype(BF16)
+        y = dot(normed, w_ref[...])
+        scale = jnp.where(lax.broadcasted_iota(jnp.int32, y.shape, 1) < feats, HD**-0.5, 1.0)
+        y = (y.astype(BF16).astype(F32) * scale).astype(BF16)
+        yt = y.T
+        spots = [(0, pl.multiple_of(slot * half, 128), half)]
+        for j in range(lay.cont_count):
+            first = lay.spread * half + j * lay.spread * lay.cont_rows
+            spots.append(
+                (
+                    half + j * lay.cont_rows,
+                    pl.multiple_of(first + slot * lay.cont_rows, 128),
+                    lay.cont_rows,
+                )
+            )
+        for start, to, size in spots:
+            h1_ref[pl.ds(to, size)] = normed[start : start + size]
+            qkvt_ref[:, pl.ds(to, size)] = yt[:, start : start + size]
+            for i in range(3 * heads):
+                qkvn_ref[i, pl.ds(to, size)] = y[start : start + size, i * HD : (i + 1) * HD]
 
     @pl.when(h == 0)
     def _():
-        for block in range(lay.blocks):
-            base = block * BK
-            for c, start, at, size in lay.pieces[block]:
-                x = x_ref[c, start : start + size].astype(F32)
-                r = lax.rsqrt(jnp.mean(x * x, axis=1, keepdims=True) + EPSILON)
-                h1_ref[base + at : base + at + size] = (x * r * gain_ref[...]).astype(BF16)
-            y = dot(h1_ref[base : base + BK], w_ref[...]).astype(BF16)
-            scale = jnp.where(lax.broadcasted_iota(jnp.int32, y.shape, 1) < heads * HD, HD**-0.5, 1.0)
-            y = (y.astype(F32) * scale).astype(BF16)
-            yt = y.T
-            qkvt_ref[:, base : base + BK] = yt
-            for i in range(3 * heads):
-                qkvn_ref[i, base : base + BK] = y[:, i * HD : (i + 1) * HD]
-
-    table_row = tab_ref[0]
+        greet(
+            [{"context": t} for t in (near, across, far)]
+            + [{"expert": flip(expert, k)} for k in range(1, peers)]
+        )
+        x_all[me, :half] = xp_ref[...]
+        x_all[me, half:] = xc_ref[...]
+        for part in range(2):
+            x_copy(me, part, part, across).start()
+        for part in range(2):
+            x_copy(me, part, 2 + part, near).start()
+        tokens = lay.tokens
+        lane = lax.broadcasted_iota(jnp.int32, (tokens, 128), 1)
+        routes = jnp.concatenate([rp_ref[...], rc_ref[...]], axis=0).astype(F32)
+        routes = jnp.where(lane == 0, routes[:, 0:1], routes[:, 1:2])
+        cols, rows, hots = make_plan(capacity, routes, order_ref[...])
+        cols_ref[...] = cols
+        rows_ref[...] = rows
+        dz = jnp.concatenate([zp_ref[...], zc_ref[...]], axis=0)
+        for k in list(range(1, peers)) + [0]:
+            base = flip(expert, k) * capacity
+            number = (lax.broadcasted_iota(jnp.int32, (capacity, tokens), 0) + base).astype(F32)
+            first = jnp.where(rows[0:1] == number, 1.0, 0.0)
+            second = jnp.where(rows[1:2] == number, 1.0, 0.0)
+            dz_scr[k, :, :width] = dot((first + second).astype(BF16), dz).astype(BF16)
+            other = dot(first.astype(BF16), hots[1].astype(BF16))
+            other = other + dot(second.astype(BF16), hots[0].astype(BF16))
+            dz_scr[k, :, width:] = other.astype(BF16)
+            if k:
+                z_copy(k).start()
+            else:
+                z_own.start()
+        for c in range(lay.spread):
+
+            @pl.when(me == c)
+            def _():
+                for i, ref in enumerate((wq_ref, wk_ref, wv_ref)):
+                    w_ref[:, i * feats : (i + 1) * feats] = ref[:, c * feats : (c + 1) * feats]
+
+        project(me)
+        for part in range(2):
+            x_copy(near, part, 2 + part, near).wait_recv()
+        project(near)
+        for part in range(2):
+            x_copy(across, part, part, across).wait_recv()
+            x_copy(across, part, 4 + part, near).start()
+        project(across)
+        for part in range(2):
+            x_copy(far, part, 4 + part, near).wait_recv()
+        project(far)
+        for part in range(2):
+            x_copy(me, part, part, across).wait_send()
+            x_copy(me, part, 2 + part, near).wait_send()
+            x_copy(across, part, 4 + part, near).wait_send()
+
+    column = lax.broadcasted_iota(jnp.int32, bias_ref.shape, 1) == me * heads + h
+    column = jnp.sum(jnp.where(column, bias_ref[...], 0.0), axis=1, keepdims=True)
+    span = buckets_ref.shape[1]
+    number = lax.broadcasted_iota(jnp.int32, (bias_ref.shape[0], span), 0)
+    table_row = jnp.sum(
+        jnp.where(buckets_ref[...] == number, column, 0.0), axis=0, keepdims=True
+    )
+    table_row = jnp.concatenate([jnp.zeros((1, BK), F32), table_row], axis=1)
     for d in range(lay.distances):
         bias_scr[d] = toeplitz_tile(table_row, d)
     hrow = pl.multiple_of(h * HD, HD)
+    vrow = pl.multiple_of(2 * feats + h * HD, HD)
     for q in range(lay.blocks):
         qt = qkvt_ref[pl.ds(hrow, HD), q * BK : (q + 1) * BK]
         top = None
@@ -206,7 +336,6 @@
             m = jnp.max(s, axis=0, keepdims=True)
             top = m if top is None else jnp.maximum(top, m)
         total, out = 0.0, 0.0
-        vrow = pl.multiple_of(2 * heads * HD + h * HD, HD)
         for n, k in enumerate(lay.keys[q]):
             e = jnp.exp(s_scr[n] - top)
             total = total + jnp.sum(e, axis=0, keepdims=True)
@@ -218,21 +347,32 @@
         out = out * inverse
         ot_ref[pl.ds(hrow, HD), q * BK : (q + 1) * BK] = out
         for c, start, at, size in lay.pieces[q]:
-            at_ref[c, pl.ds(hrow, HD), start : start + size] = out[:, at : at + size].astype(BF16)
-
-
-def attention_forward(lay, heads, x_all, gain, weights, table):
-    width = x_all.shape[2]
+            at_scr[c, pl.ds(hrow, HD), start : start + size] = out[:, at : at + size].astype(BF16)
+
+    for k in (3, 2, 1):
+        a_copy(k, h).start()
+    a_own(h).start()
+
+    @pl.when(h == heads - 1)
+    def _():
+        for head in range(heads):
+            a_own(head).wait()
+            for k in (1, 2, 3):
+                a_copy(k, head).wait()
+        z_own.wait()
+        for k in range(1, peers):
+            z_copy(k).wait()
+
+
+def front(lay, heads, peers, capacity, *args):
+    width = args[0].shape[1]
     feats = heads * HD
+    dma = pltpu.SemaphoreType.DMA
+    anywhere = pl.BlockSpec(memory_space=pl.ANY)
     return pl.pallas_call(
-        functools.partial(attention_kernel, lay, heads),
+        functools.partial(front_kernel, lay, heads, peers, capacity),
         grid=(heads,),
-        in_specs=[
-            full(x_all.shape),
-            full((1, width)),
-            full(weights.shape),
-            pl.BlockSpec((1, 1, table.shape[2]), lambda h: (h, 0, 0)),
-        ],
+        in_specs=[full(a.shape) for a in args],
         out_specs=(
             full((lay.total, width)),
             full((3 * heads, lay.total, HD)),
@@ -240,7 +380,11 @@
             pl.BlockSpec((1, lay.tiles, BK, BK), lambda h: (h, 0, 0, 0)),
             full((feats, lay.total)),
             pl.BlockSpec((1, 1, lay.total), lambda h: (h, 0, 0)),
-            full((lay.spread, feats, lay.tokens)),
+            full((width, 3 * feats)),
+            full((lay.tokens, 128)),
+            full((8, lay.tokens)),
+            anywhere,
+            anywhere,
         ),
         out_shape=(
             jax.ShapeDtypeStruct((lay.total, width), BF16),
@@ -249,15 +393,31 @@
             jax.ShapeDtypeStruct((heads, lay.tiles, BK, BK), BF16),
             jax.ShapeDtypeStruct((feats, lay.total), F32),
             jax.ShapeDtypeStruct((heads, 1, lay.total), F32),
+            jax.ShapeDtypeStruct((width, 3 * feats), BF16),
+            jax.ShapeDtypeStruct((lay.tokens, 128), F32),
+            jax.ShapeDtypeStruct((8, lay.tokens), F32),
             jax.ShapeDtypeStruct((lay.spread, feats, lay.tokens), BF16),
+            jax.ShapeDtypeStruct((peers, capacity, width + 128), BF16),
         ),
         scratch_shapes=[
+            VMEM((lay.spread, lay.tokens, width), BF16),
+            VMEM((lay.spread, feats, lay.tokens), BF16),
+            VMEM((peers, capacity, width + 128), BF16),
             VMEM((max(len(k) for k in lay.keys), BK, BK), F32),
             VMEM((lay.distances, BK, BK), F32),
+            dma((6,)),
+            dma((6,)),
+            dma((heads, 4)),
+            dma((heads, 4)),
+            dma((peers,)),
+            dma((peers,)),
+            dma,
         ],
-        compiler_params=pltpu.CompilerParams(vmem_limit_bytes=58 * MIB),
-        name="attention_forward",
-    )(x_all, gain, weights, table)
+        compiler_params=pltpu.CompilerParams(
+            vmem_limit_bytes=60 * MIB, collective_id=0, has_side_effects=True
+        ),
+        name="front",
+    )(*args)
 
 
 def middle_kernel(
@@ -677,30 +837,39 @@
             axis=0,
         )
 
-    def own_columns(matrix):
-        return lax.dynamic_slice_in_dim(matrix, context * feats, feats, 1)
-
     def exchange(array, axis):
         return lax.all_to_all(array, axis, split_axis=0, concat_axis=0, tiled=True)
 
     x_local = local_rows(prompt_in, cont_in)
-    x_all = lax.all_gather(x_local, "context", axis=0, tiled=False)
     routes = local_rows(prompt_route, cont_route)
     upstream = local_rows(prompt_cot, cont_cot)
     gain_one = attn_gain.reshape(1, width)
     gain_two = ffn_gain.reshape(1, width)
-    slot_rows, slot_cols, dz_slots = plan(routes, order.reshape(tokens), upstream, experts, capacity)
-    dz_slots = exchange(dz_slots.reshape(expert_devices, slots // expert_devices, -1), "expert")
-    dz_slots = dz_slots.reshape(slots, -1)
-
+    h1, qkvn, qkvt, e, ot, rl, weights, cols, rows, at, dz_slots = front(
+        lay,
+        heads,
+        expert_devices,
+        capacity,
+        prompt_in.reshape(prompt_rows, width),
+        cont_in.reshape(cont_count * cont_rows, width),
+        prompt_route.reshape(prompt_rows, 2),
+        cont_route.reshape(cont_count * cont_rows, 2),
+        order.reshape(1, tokens),
+        buckets.reshape(1, -1),
+        gain_one,
+        w_query,
+        w_key,
+        w_value,
+        rel_bias,
+        prompt_cot.reshape(prompt_rows, width),
+        cont_cot.reshape(cont_count * cont_rows, width),
+    )
+    slot_cols, slot_rows = cols.astype(jnp.int32), rows.astype(jnp.int32)
+    turned = jnp.arange(expert_devices, dtype=jnp.int32) ^ lax.axis_index("expert")
+    dz_slots = dz_slots[turned].reshape(slots, -1)
+    attended_t = at.reshape(width, tokens)
     bucket_hot = (buckets[:, None] == jnp.arange(buckets_count, dtype=jnp.int32)[None, :]).astype(F32)
-    own_bias = lax.dynamic_slice_in_dim(rel_bias, context * heads, heads, 1)
-    table = jnp.dot(bucket_hot, own_bias, precision=PRECISE).T
-    table = jnp.pad(table, ((0, 0), (BK, 0))).reshape(heads, 1, -1)
-    weights = jnp.concatenate([own_columns(w) for w in (w_query, w_key, w_value)], axis=1)
     weights_t = weights.T
-    h1, qkvn, qkvt, e, ot, rl, at = attention_forward(lay, heads, x_all, gain_one, weights, table)
-    attended_t = exchange(at, "context").reshape(width, tokens)
     mid, h2, gates, sent = middle(
         attended_t, x_local, w_attn_out, gain_two, router, routes, slot_rows, experts, capacity
     )

time: 785 us -> 617 us (0.79)
  blocking collectives: 162 us -> 50.3 us
  waiting for transfers between devices: 406 us -> 308 us
  Pallas kernels: 126 us -> 155 us
    all_to_all x4 -> x1, blocking collectives: 122 us -> 9.19 us  [exchange(): return lax.all_to_all(array, axis, split_axis=0, concat_axis=0, tiled=True)]
    reduce_scatter x2, waiting for transfers between devices: 63.6 us -> 0.03 us  [body(): lax.psum_scatter(g, ('dp', 'context'), scatter_dimension=1, tiled=True)]
    all_to_all x3 -> x4, waiting for transfers between devices: 80.5 us -> 127 us  [exchange(): return lax.all_to_all(array, axis, split_axis=0, concat_axis=0, tiled=True)]
    psum x1, waiting for transfers between devices: 127 us -> 81 us  [body(): g_wo, small = lax.psum((g_wo, small), ('dp', 'context', 'expert'))]
    pallas_call x2 -> x1, Pallas kernels: 28.7 us -> 58.1 us  [front(): pl.pallas_call(functools.partial(front_kernel, lay, heads, peers, capacit...]
    all_gather x1 -> x0, waiting for transfers between devices: 24.9 us -> none  [body(): x_all = lax.all_gather(x_local, 'context', axis=0, tiled=False)]
    reduce_scatter x1, waiting for transfers between devices: 38.3 us -> 21.1 us  [body(): dh1 = lax.psum_scatter(dh1, 'context', scatter_dimension=0, tiled=False)]
    all_to_all x3 -> x4, starting transfers between devices: 13 us -> 19.2 us  [exchange(): return lax.all_to_all(array, axis, split_axis=0, concat_axis=0, tiled=True)]
  transfers between devices with their start and end apart: 10 -> 10, of which waited for: 10 -> 8; matrix products, arithmetic and copies ran while one was open for 4% -> 5% of each run, Pallas kernels for 4% -> 5%
where the time goes in v2:
time: 617 us; the launch traced here: 607 us
  waiting for transfers between devices  308 us (50%)
  Pallas kernels  155 us (25%)
  blocking collectives  50.3 us (8%)
  local copies, waits for them, and re-layouts  48.7 us (8%)
  starting transfers between devices  19.7 us (3%)
  between operations  16.3 us (3%)
  other arithmetic  7.59 us (1%)
    all_to_all x4, waiting for transfers between devices, exchange(): return lax.all_to_all(array, axis, split_axis=0, concat_axis=0, tiled=True)  127 us
    psum x1, waiting for transfers between devices, body(): g_wo, small = lax.psum((g_wo, small), ('dp', 'context', 'expert'))  81 us
    psum x1, waiting for transfers between devices, body(): g_qkv = lax.psum(g_qkv, ('dp', 'expert'))  73.3 us
    pallas_call x1, Pallas kernels, front(): pl.pallas_call(functools.partial(front_kernel, lay, heads, peers, capacit...  58.1 us
    psum x1, blocking collectives, body(): g_wo, small = lax.psum((g_wo, small), ('dp', 'context', 'expert'))  41.1 us
    pallas_call x1, Pallas kernels, attention_backward(): pl.pallas_call(functools.partial(attention_back_kernel, lay, heads), grid...  29.9 us
    pallas_call x1, Pallas kernels, expert_grad(): pl.pallas_call(functools.partial(expert_grad_kernel, steps), grid=(steps,...  28.6 us
    unnamed x64, local copies, waits for them, and re-layouts  28 us
  transfers between devices with their start and end apart: 10, of which 8 were waited for; matrix products, arithmetic and copies ran while one was open for 5% of the time, Pallas kernels for 5%

profile of v2, /device:TPU:0, one launch (start us, length us, event | category | flops | bytes accessed | tf_op | source)
XLA Modules:
  0.0 606.5 jit_solution(10409755229998540879)
XLA Ops:
  14.9 58.1 %front.1 = (bf16[2048,768]{1,0:T(8,128)(2,1)}, bf16[9,2048,64]{2,1,0:T(8,128)(2,1)}, bf16[576,2048]{1,0:T(8,128)(2,1)}, bf16[3,32,256,256]{3,2,1,0:T(8,128)(2,1)...) custom-call(bf16[256,768]{1,0:T(8,128)(2,1)} %bitcast.60, ...), custom_call_target="tpu_custom_call" | custom-call | tf_op jit(solution)/shard_map/front/pallas_call | solution.py:372
  75.2 3.1 middle.1
  81.6 7.3 %all-to-all-start = ((bf16[4,288,768]{2,1,0:T(8,128)(2,1)}), bf16[4,288,768]{2,1,0:T(8,128)(2,1)}, u32[]{:S(2)}, u32[]{:S(2)}) async-start(bf16[4,288,768]{2,1,0:T(8,128)(2,1)} %bitcast.47), calls=%async_computation | async-start | bytes 3538944 | tf_op jit(solution)/shard_map/all_to_all | solution.py:841
  88.9 3.7 gather_fusion
  92.6 37.5 %all-to-all-done = bf16[4,288,768]{2,1,0:T(8,128)(2,1)} async-done(((bf16[4,288,768]{2,1,0:T(8,128)(2,1)}), bf16[4,288,768]{2,1,0:T(8,128)(2,1)}, u32[]{:S(2)}, u32[]{:S(2)}) %all-to-all-start) | async-done | bytes 1769504 | tf_op jit(solution)/shard_map/all_to_all | solution.py:841
  130.1 28.6 %expert_grad.1 = (bf16[1152,3072]{1,0:T(8,128)(2,1)}, bf16[1152,3072]{1,0:T(8,128)(2,1)}, bf16[1152,768]{1,0:T(8,128)(2,1)}, bf16[1152,768]{1,0:T(8,128)(2,1)}, f32[1152,128]{1,0:T(8,128)}) custom-call(bf16[1152,768]{1,0:T(8,128)(2,1)} %bitcast.9.sent_ref, bf16[1152,896]{1,0:T(8,128)(2,1)} %bitcast.53, bf16[768,4]{1,0:T(8,128)(2,1)} %copy-done.5, ...), custom_call_target="tpu_custom_call" | custom-call | tf_op jit(solution)/shard_map/expert_grad/pallas_call | solution.py:524
  160.1 9.2 %all_to_all.30 = f32[4,1,288]{2,1,0:T(1,128)S(1)} all-to-all(f32[4,1,288]{2,1,0:T(1,128)S(1)} %all_to_all.24), channel_id=1, replica_groups=mesh['dp'=2,'context'=4,'expert'=4] {'expert'}, dimensions={0} | all-to-all | bytes 9216 | tf_op jit(solution)/shard_map/all_to_all | solution.py:841
  169.3 4.5 all-to-all-start.2
  175.3 37.8 %all-to-all-done.2 = bf16[4,288,768]{2,1,0:T(8,128)(2,1)} async-done(((bf16[4,288,768]{2,1,0:T(8,128)(2,1)}), bf16[4,288,768]{2,1,0:T(8,128)(2,1)}, u32[]{:S(2)}, u32[]{:S(2)}) %all-to-all-start.2) | async-done | bytes 1769504 | tf_op jit(solution)/shard_map/all_to_all | solution.py:841
  216.3 8.1 %turn.1 = (f32[512,768]{1,0:T(8,128)}, bf16[768,512]{1,0:T(8,128)(2,1)S(1)}, f32[768,768]{1,0:T(8,128)}, f32[1,768]{1,0:T(1,128)S(1)}, f32[4,768]{1,0:T(4,128)S(1)}) custom-call(bf16[1152,768]{1,0:T(8,128)(2,1)} %bitcast.17.dsent_ref, f32[1,1152]{1,0:T(1,128)S(1)} %reshape.150.share_ref, s32[512,128]{1,0:T(8,128)S(1)} %convert_element_type.16.cols_ref, ...), custom_call_target="tpu_custom_call" | custom-call | tf_op jit(solution)/shard_map/turn/pallas_call | solution.py:638
  225.3 3.6 all-to-all-start.4
  229.0 1.4 copy.92
  230.5 10.1 %all-to-all-done.4.dot_ref = bf16[4,192,512]{2,1,0:T(8,128)(2,1)S(1)} async-done(((bf16[4,192,512]{2,1,0:T(8,128)(2,1)}), bf16[4,192,512]{2,1,0:T(8,128)(2,1)S(1)}, u32[]{:S(2)}, u32[]{:S(2)}) %all-to-all-start.4) | async-done | bytes 786464 | tf_op jit(solution)/shard_map/all_to_all | solution.py:841
  241.5 29.9 %attention_backward.1 = (bf16[4,512,768]{2,1,0:T(8,128)(2,1)}, f32[576,768]{1,0:T(8,128)}, f32[3,1,1792]{2,1,0:T(1,128)}) custom-call(bf16[4,192,512]{2,1,0:T(8,128)(2,1)} %copy-done.19, bf16[3,32,256,256]{3,2,1,0:T(8,128)(2,1)} %get-tuple-element.62.e_ref, bf16[9,2048,64]{2,1,0:T(8,128)(2,1)} %get-tuple-element.63.qkvn_ref, ...), custom_call_target="tpu_custom_call" | custom-call | tf_op jit(solution)/shard_map/attention_backward/pallas_call | solution.py:721
  271.4 24.4 %expert_weights.1 = (bf16[1152,768]{1,0:T(8,128)(2,1)}, bf16[1,768,3072]{2,1,0:T(8,128)(2,1)}, bf16[1,3072,768]{2,1,0:T(8,128)(2,1)}) custom-call(bf16[1152,768]{1,0:T(8,128)(2,1)} %bitcast.9.sent_ref, bf16[1152,768]{1,0:T(8,128)(2,1)} %get-tuple-element.54.dmade_ref, bf16[1152,3072]{1,0:T(8,128)(2,1)} %get-tuple-element.55.act_ref, ...), custom_call_target="tpu_custom_call" | custom-call | tf_op jit(solution)/shard_map/expert_weights/pallas_call | solution.py:577
  297.1 73.3 %all-reduce.4.cloned.1.call-done = f32[1,576,768]{2,1,0:T(8,128)} async-done(((f32[1,576,768]{2,1,0:T(8,128)}), f32[1,576,768]{2,1,0:T(8,128)}) %all-reduce.4.cloned.1.call-update) | async-done | bytes 1769488 | tf_op jit(solution)/shard_map/psum | solution.py:915
  370.4 3.7 all-to-all-start.1
  374.4 41.4 %all-to-all-done.1 = bf16[4,288,768]{2,1,0:T(8,128)(2,1)S(1)} async-done(((bf16[4,288,768]{2,1,0:T(8,128)(2,1)}), bf16[4,288,768]{2,1,0:T(8,128)(2,1)S(1)}, u32[]{:S(2)}, u32[]{:S(2)}) %all-to-all-start.1) | async-done | bytes 1769504 | tf_op jit(solution)/shard_map/all_to_all | solution.py:841
  415.8 1.7 copy-done.1
  417.5 2.2 result.1
  421.6 2.2 convert_element_type.17
  423.8 2.2 convert_element_type.18
  425.9 21.1 %reduce-scatter.4.cloned.1.call-done = bf16[1,512,768]{2,1,0:T(8,128)(2,1)} async-done(((bf16[4,512,768]{2,1,0:T(8,128)(2,1)}), bf16[1,512,768]{2,1,0:T(8,128)(2,1)}) %reduce-scatter.4.cloned.1.call-update) | async-done | bytes 786448 | tf_op jit(solution)/shard_map/reduce_scatter | solution.py:905
  450.1 41.1 %psum.21 = f32[18,768]{1,0:T(8,128)S(1)} all-reduce(f32[18,768]{1,0:T(8,128)S(1)} %pad_maximum_fusion.2), channel_id=1, replica_groups=mesh['dp'=2,'context'=4,'expert'=4] {'dp','context','expert'}, use_global_device_ids=true, to_apply=%region_1.0 | all-reduce | flops 13824 | bytes 110592 | tf_op jit(solution)/shard_map/psum | solution.py:914
  493.0 2.6 fusion.6
  495.6 4.9 all-gather.2.cloned.1.call-done
  500.5 5.9 fusion.5
  506.4 3.0 copy.93
  509.4 3.0 copy.94
  512.5 1.9 copy.95
  514.4 81.0 %all-reduce.6.cloned.1.call-done = f32[768,768]{1,0:T(8,128)} async-done(((f32[768,768]{1,0:T(8,128)}), f32[768,768]{1,0:T(8,128)}) %all-reduce.6.cloned.1.call-update) | async-done | bytes 2359312 | tf_op jit(solution)/shard_map/psum | solution.py:914
  595.5 3.2 copy.104
  (98 shorter events, 28.3 us)
Async XLA Ops:
  8.8 6.0 copy-start.20
  9.7 5.2 copy-start.21
  14.9 59.1 %copy-start.9 = (s32[512,2]{1,0:T(8,128)}, s32[512,2]{1,0:T(8,128)S(1)}, u32[]{:S(2)}) copy-start(s32[512,2]{1,0:T(8,128)S(1)} %pad_add_fusion.route_ref) | copy-start | bytes 12292
  14.9 58.9 %copy-start.26 = (bf16[768,4]{0,1:T(4,128)(2,1)S(1)}, bf16[768,4]{0,1:T(4,128)(2,1)}, u32[]{:S(2)}) copy-start(bf16[768,4]{0,1:T(4,128)(2,1)} %param.31) | copy-start | bytes 18436
  14.9 59.0 %copy-start.27 = (f32[768]{0:T(1024)S(1)}, f32[768]{0:T(1024)}, u32[]{:S(2)}) copy-start(f32[768]{0:T(1024)} %param.30) | copy-start | bytes 9220
  14.9 59.1 %copy-start.2 = (bf16[768,768]{1,0:T(8,128)(2,1)S(1)}, bf16[768,768]{1,0:T(8,128)(2,1)}, u32[]{:S(2)}) copy-start(bf16[768,768]{1,0:T(8,128)(2,1)} %wo_ref.3) | copy-start | bytes 3538948
  73.9 7.7 %copy-start.5 = (bf16[768,4]{1,0:T(8,128)(2,1)}, bf16[768,4]{1,0:T(8,128)(2,1)S(1)}, u32[]{:S(2)}) copy-start(bf16[768,4]{1,0:T(8,128)(2,1)S(1)} %copy.88.router_ref) | copy-start | bytes 18436
  74.0 1.2 copy-start.3
  78.3 1.2 copy-start
  79.5 1.2 copy-start.11
  81.6 48.5 %all-to-all-start = ((bf16[4,288,768]{2,1,0:T(8,128)(2,1)}), bf16[4,288,768]{2,1,0:T(8,128)(2,1)}, u32[]{:S(2)}, u32[]{:S(2)}) async-start(bf16[4,288,768]{2,1,0:T(8,128)(2,1)} %bitcast.47), calls=%async_computation | async-start | bytes 3538944 | tf_op jit(solution)/shard_map/all_to_all | solution.py:841
  158.7 15.2 %copy-start.23 = (f32[512,128]{1,0:T(8,128)S(1)}, f32[512,128]{1,0:T(8,128)}, u32[]{:S(2)}) copy-start(f32[512,128]{1,0:T(8,128)} %get-tuple-element.50) | copy-start | bytes 786436
  169.3 43.8 %copy-start.6 = (bf16[768,4]{1,0:T(8,128)(2,1)S(1)}, bf16[768,4]{1,0:T(8,128)(2,1)}, u32[]{:S(2)}) copy-start(bf16[768,4]{1,0:T(8,128)(2,1)} %copy-done.5) | copy-start | bytes 18436
  169.3 43.8 %all-to-all-start.2 = ((bf16[4,288,768]{2,1,0:T(8,128)(2,1)}), bf16[4,288,768]{2,1,0:T(8,128)(2,1)}, u32[]{:S(2)}, u32[]{:S(2)}) async-start(bf16[4,288,768]{2,1,0:T(8,128)(2,1)} %bitcast.58), calls=%async_computation.2 | async-start | bytes 3538944 | tf_op jit(solution)/shard_map/all_to_all | solution.py:841
  173.9 50.5 %copy-start.7 = (s32[512,128]{1,0:T(8,128)}, s32[512,128]{1,0:T(8,128)S(1)}, u32[]{:S(2)}) copy-start(s32[512,128]{1,0:T(8,128)S(1)} %convert_element_type.16.cols_ref) | copy-start | bytes 786436
  213.1 1.1 copy-start.4
  215.2 1.1 copy-start.15
  225.3 3.7 copy-start.22
  225.3 15.3 %all-to-all-start.4 = ((bf16[4,192,512]{2,1,0:T(8,128)(2,1)}), bf16[4,192,512]{2,1,0:T(8,128)(2,1)S(1)}, u32[]{:S(2)}, u32[]{:S(2)}) async-start(bf16[4,192,512]{2,1,0:T(8,128)(2,1)} %bitcast.48), calls=%async_computation.4 | async-start | bytes 1572864 | tf_op jit(solution)/shard_map/all_to_all | solution.py:841
  229.0 141.4 %all-reduce.4.cloned.1.call-start = ((), (), s32[]{:S(2)}) async-start(), calls=%async_computation.9 | async-start | bytes 3538944 | tf_op jit(solution)/shard_map/psum | solution.py:915
  271.4 150.2 %reduce-scatter.6.cloned.1.call-start = ((), (), s32[]{:S(2)}) async-start(), calls=%async_computation.12 | async-start | bytes 5308416 | tf_op jit(solution)/shard_map/reduce_scatter | solution.py:899
  295.9 127.9 %reduce-scatter.8.cloned.1.call-start = ((), (), s32[]{:S(2)}) async-start(), calls=%async_computation.13 | async-start | bytes 5308416 | tf_op jit(solution)/shard_map/reduce_scatter | solution.py:899
  296.5 150.5 %reduce-scatter.4.cloned.1.call-start = ((), (), s32[]{:S(2)}) async-start(), calls=%async_computation.8 | async-start | bytes 3932160 | tf_op jit(solution)/shard_map/reduce_scatter | solution.py:905
  297.0 203.5 %all-gather.2.cloned.1.call-start = ((), (), s32[]{:S(2)}) async-start(), calls=%async_computation.10 | async-start | bytes 8847360 | tf_op jit(solution)/shard_map/all_gather | solution.py:916
  370.4 45.4 %copy-start.8 = (s32[512,128]{1,0:T(8,128)S(1)}, s32[512,128]{1,0:T(8,128)}, u32[]{:S(2)}) copy-start(s32[512,128]{1,0:T(8,128)} %copy-done.7) | copy-start | bytes 786436
  370.4 45.4 %all-to-all-start.1 = ((bf16[4,288,768]{2,1,0:T(8,128)(2,1)}), bf16[4,288,768]{2,1,0:T(8,128)(2,1)S(1)}, u32[]{:S(2)}, u32[]{:S(2)}) async-start(bf16[4,288,768]{2,1,0:T(8,128)(2,1)} %bitcast.56), calls=%async_computation.1 | async-start | bytes 3538944 | tf_op jit(solution)/shard_map/all_to_all | solution.py:841
  374.1 221.3 %all-reduce.6.cloned.1.call-start = ((), (), s32[]{:S(2)}) async-start(), calls=%async_computation.11 | async-start | bytes 4718592 | tf_op jit(solution)/shard_map/psum | solution.py:914
  415.8 1.7 copy-start.1
  420.7 26.3 %copy-start.12 = (f32[512,768]{1,0:T(8,128)S(1)}, f32[512,768]{1,0:T(8,128)}, u32[]{:S(2)}) copy-start(f32[512,768]{1,0:T(8,128)} %get-tuple-element.70.dmid_ref) | copy-start | bytes 4718596
  420.7 26.2 %copy-start.18 = (f32[1,768]{1,0:T(1,128)S(1)}, f32[1,768]{1,0:T(1,128)}, u32[]{:S(2)}) copy-start(f32[1,768]{1,0:T(1,128)} %reshape.136.gain_ref) | copy-start | bytes 9220
  447.0 1.1 copy-start.17
  449.0 1.1 copy-start.13
  (6 other events, 5.6 us)
Sparse Core Ops, SparseCore 0:
  271.5 98.8 all-reduce.3
  420.8 174.5 all-reduce.5
Sparse Core Ops, SparseCore 1:
  296.0 52.1 reduce-scatter.5
  351.8 53.7 reduce-scatter.7
  408.0 38.9 reduce-scatter.3
  448.5 51.9 all-gather.1
